TPU v7x, 32 devices: a whole 2x2x4 slice. The times are simulated.
32 devices in a mesh: expert: 4 (over z), etp: 2 (over x), tp: 4 (over y, core).
Axes of the slice: x: 2, y: 2, z: 4, core: 2. Of those that a mesh axis runs over, the one named last changes fastest.
Arguments:
- d_out: bfloat16 [2048, 6144], P(('expert', 'tp'), 'etp'), may hold values from -6 to 6
- expert_ids: int32 [2048, 2], P(('expert', 'tp')), may hold values from 0 to 3, all different within a row; in each aligned block of 128 rows (0 to 127, 128 to 255, ...) at most 64 rows name the same one
- gate_weights: float32 [2048, 2], P(('expert', 'tp')), may hold values from 0.05 to 0.95, as said below
- saved_gate: bfloat16 [4, 1024, 16384], P('expert', None, ('etp', 'tp')), may hold values from -8 to 8
- saved_up: bfloat16 [4, 1024, 16384], P('expert', None, ('etp', 'tp')), may hold values from -6 to 6
- w_gate: bfloat16 [4, 6144, 16384], P('expert', None, ('etp', 'tp')), may hold values from -0.078125 to 0.078125
- w_up: bfloat16 [4, 6144, 16384], P('expert', None, ('etp', 'tp')), may hold values from -0.078125 to 0.078125
- w_down: bfloat16 [4, 16384, 6144], P('expert', ('etp', 'tp')), may hold values from -0.046875 to 0.046875
- w_out: bfloat16 [6144, 6144], P('tp', 'etp'), may hold values from -0.078125 to 0.078125
Outputs:
- d_hidden: bfloat16 [2048, 6144], P(('expert', 'tp'), 'etp')
- d_heads: bfloat16 [2048, 6144], P(('expert', 'etp'), 'tp')
Inputs may be any that keep to these rules, and one draw needn't show every extreme that they name: `expert_ids`: each token names two different experts; in every block of 128 tokens every expert is named by exactly 64 tokens. `gate_weights`: a token's two weights sum to one.
All inputs are finite; a program needn't handle non-finite values.
Results may differ from a plain program's by a relative error of at most 0.02.
Values may be sent and summed in bfloat16 or wider, within the bound.
A program may use at most 192 MiB of HBM per device.

v0:
```python
import jax
import jax.numpy as jnp
from jax import lax
from jax.sharding import PartitionSpec as P


def body(d_out, expert_ids, gate_weights, saved_gate, saved_up, w_gate, w_up, w_down, w_out):
    expert_count = lax.axis_size("expert")
    tp_count = lax.axis_size("tp")
    feat_local = d_out.shape[1]
    cap_slots = saved_gate.shape[1] // (expert_count * tp_count)
    model_width = w_gate.shape[1]
    experts_iota = jnp.arange(expert_count, dtype=jnp.int32)
    first_hit = expert_ids[:, 0:1] == experts_iota[None, :]
    second_hit = expert_ids[:, 1:2] == experts_iota[None, :]
    member = first_hit.astype(jnp.int32) + second_hit.astype(jnp.int32)
    weight = gate_weights[:, 0:1] * first_hit.astype(jnp.float32) + gate_weights[
        :, 1:2
    ] * second_hit.astype(jnp.float32)
    slot = jnp.cumsum(member, axis=0) - member
    slot_iota = jnp.arange(cap_slots, dtype=jnp.int32)
    select = ((slot[:, :, None] == slot_iota[None, None, :]) & (member[:, :, None] > 0)).astype(
        jnp.float32
    )
    weighted_sel = select * weight[:, :, None]
    outgoing = jnp.einsum(
        "tec,td->ecd", weighted_sel, d_out.astype(jnp.float32), precision=lax.Precision.HIGHEST
    ).astype(jnp.bfloat16)
    received = lax.all_to_all(outgoing, "expert", split_axis=0, concat_axis=0, tiled=True)
    blocks_all = lax.all_gather(received[:, None], "tp", axis=1, tiled=True)
    down_local = w_down[0]
    slot_rows = blocks_all.shape[0] * blocks_all.shape[1] * blocks_all.shape[2]
    shard_piece = lax.all_gather(blocks_all, "etp", axis=3, tiled=True)
    width_piece = shard_piece.shape[3]
    flat_rows = shard_piece.reshape(slot_rows, width_piece)
    grad_act = lax.dot_general(
        flat_rows, down_local, (((1,), (1,)), ((), ())), preferred_element_type=jnp.float32
    )
    gate_val = saved_gate[0].astype(jnp.float32)
    up_val = saved_up[0].astype(jnp.float32)
    sigma = jax.nn.sigmoid(gate_val)
    grad_up = (grad_act * gate_val * sigma).astype(jnp.bfloat16)
    grad_gate = (grad_act * up_val * sigma * (1.0 + gate_val * (1.0 - sigma))).astype(jnp.bfloat16)
    gate_local = w_gate[0]
    up_local = w_up[0]
    first_part = lax.dot_general(
        gate_local, grad_gate, (((1,), (1,)), ((), ())), preferred_element_type=jnp.float32
    )
    whole_term = (
        first_part
        + lax.dot_general(
            up_local, grad_up, (((1,), (1,)), ((), ())), preferred_element_type=jnp.float32
        )
    ).reshape(model_width, expert_count, tp_count, cap_slots)
    by_block = lax.psum_scatter(
        whole_term.astype(jnp.bfloat16), "tp", scatter_dimension=2, tiled=True
    )
    reduced = lax.psum_scatter(by_block, "etp", scatter_dimension=0, tiled=True).astype(jnp.float32)
    returned = lax.all_to_all(
        reduced.reshape(feat_local, expert_count, cap_slots).astype(jnp.bfloat16),
        "expert",
        split_axis=1,
        concat_axis=1,
        tiled=True,
    ).astype(jnp.float32)
    d_moe = jnp.einsum("tec,dec->td", select, returned, precision=lax.Precision.HIGHEST)
    d_hidden = (d_out.astype(jnp.float32) + d_moe).astype(jnp.bfloat16)
    head_partial = lax.dot_general(
        lax.all_gather(d_hidden, "tp", axis=0, tiled=True),
        w_out,
        (((1,), (1,)), ((), ())),
        preferred_element_type=jnp.float32,
    )
    d_heads = lax.psum_scatter(
        head_partial.astype(jnp.bfloat16), "etp", scatter_dimension=0, tiled=True
    )
    return (d_hidden, d_heads)


def solution(mesh):
    in_specs = (
        P(("expert", "tp"), "etp"),
        P(("expert", "tp"), None),
        P(("expert", "tp"), None),
        P("expert", None, ("etp", "tp")),
        P("expert", None, ("etp", "tp")),
        P("expert", None, ("etp", "tp")),
        P("expert", None, ("etp", "tp")),
        P("expert", ("etp", "tp"), None),
        P("tp", "etp"),
    )
    out_specs = (P(("expert", "tp"), "etp"), P(("expert", "etp"), "tp"))
    return jax.shard_map(body, mesh=mesh, in_specs=in_specs, out_specs=out_specs, check_vma=False)
```

profile of v0, /device:TPU:0, one launch (start us, length us, event | category | flops | bytes accessed | tf_op | source)
XLA Modules:
  0.0 645.3 jit_solution(18386917269061166172)
XLA Ops:
  7.2 0.0 all-gather.9.cloned.1.call-start
  7.2 0.8 slice_bitcast_fusion.3
  8.0 0.1 fusion.37
  8.1 0.1 convert_add_fusion
  8.2 0.8 slice_bitcast_fusion.1
  8.9 0.1 copy.12
  9.0 0.2 select_add_fusion
  9.2 0.1 copy.13
  9.2 0.2 reduce_window_sum.11
  9.4 0.1 fusion.38
  9.5 0.1 copy.11
  9.6 2.5 convolution_convert_fusion
  12.1 43.2 %all_to_all.10 = bf16[4,64,3072]{2,1,0:T(8,128)(2,1)} all-to-all(bf16[4,64,3072]{2,1,0:T(8,128)(2,1)S(1)} %convolution_convert_fusion), channel_id=1, replica_groups=mesh['expert'=4,'etp'=2,'tp'=4] {'expert'}, dimensions={0} | all-to-all | bytes 3145728 | tf_op jit(solution)/shard_map/all_to_all | solution.py:29
  55.3 0.0 all-gather.9.cloned.1.call-update
  55.4 0.0 all-gather.5.cloned.1.call-start
  55.4 45.6 %all-gather.9.cloned.1.call-done = bf16[4,256,3072]{2,1,0:T(8,128)(2,1)} async-done(((bf16[4,64,3072]{2,1,0:T(8,128)(2,1)}), bf16[4,256,3072]{2,1,0:T(8,128)(2,1)}) %all-gather.9.cloned.1.call-update) | async-done | bytes 6291472 | tf_op jit(solution)/shard_map/all_gather | solution.py:30
  101.1 0.0 reduce-scatter.4.cloned.1.call-start
  101.1 154.0 %all-gather.5.cloned.1.call-done = bf16[4,4,64,6144]{3,2,1,0:T(8,128)(2,1)} async-done(((bf16[4,4,64,3072]{3,2,1,0:T(8,128)(2,1)}), bf16[4,4,64,6144]{3,2,1,0:T(8,128)(2,1)}) %all-gather.5.cloned.1.call-update) | async-done | bytes 12582928 | tf_op jit(solution)/shard_map/all_gather | solution.py:33
  255.1 34.6 %fusion.4 = f32[1024,2048]{1,0:T(8,128)} fusion(bf16[1024,6144]{1,0:T(8,128)(2,1)} %bitcast.57, bf16[1,2048,6144]{2,1,0:T(8,128)(2,1)} %param.16), kind=kOutput, calls=%fused_computation.4 | convolution fusion | flops 25769803776 | bytes 46137344 | tf_op jit(solution)/shard_map/dot_general | solution.py:36
  289.8 35.3 %fusion = f32[1024,6144]{1,0:T(8,128)} fusion(bf16[1,6144,2048]{2,1,0:T(8,128)(2,1)} %param.15, f32[1024,2048]{1,0:T(8,128)} %fusion.4, bf16[1,1024,2048]{2,1,0:T(8,128)(2,1)S(1)} %copy-done.5), kind=kOutput, calls=%fused_computation | convolution fusion | flops 25784483840 | bytes 62914560 | tf_op jit(solution)/shard_map/dot_general | solution.py:51
  325.0 51.5 %add_convert_fusion = bf16[1024,6144]{1,0:T(8,128)(2,1)} fusion(f32[1024,6144]{1,0:T(8,128)} %fusion, bf16[1,6144,2048]{2,1,0:T(8,128)(2,1)} %param.14, f32[1024,2048]{1,0:T(8,128)} %fusion.4, bf16[1,1024,2048]{2,1,0:T(8,128)(2,1)} %param.13, bf16[1,1024,2048]{2,1,0:T(8,128)(2,1)} %param.12), kind=kOutput, calls=%fused_computation.6 | convolution fusion | flops 25807552512 | bytes 79691776 | tf_op jit(solution)/shard_map/dot_general | solution.py:46
  376.6 10.9 %copy.14 = bf16[6144,4,4,64]{0,3,1,2:T(8,128)(2,1)} copy(bf16[6144,4,4,64]{0,3,2,1:T(8,128)(2,1)} %bitcast.54) | data formatting | bytes 25165824 | tf_op jit(solution)/shard_map/convert_element_type | solution.py:56
  387.5 0.0 reduce-scatter.6.cloned.1.call-start
  387.5 99.1 %reduce-scatter.4.cloned.1.call-done = bf16[6144,4,1,64]{0,3,1,2:T(8,128)(2,1)} async-done(((bf16[6144,4,4,64]{0,3,1,2:T(8,128)(2,1)}), bf16[6144,4,1,64]{0,3,1,2:T(8,128)(2,1)}) %reduce-scatter.4.cloned.1.call-update) | async-done | bytes 3145744 | tf_op jit(solution)/shard_map/reduce_scatter | solution.py:55
  486.7 0.0 all-gather.7.cloned.1.call-start
  486.7 45.4 %reduce-scatter.6.cloned.1.call-done = bf16[3072,4,1,64]{0,3,1,2:T(8,128)(2,1)} async-done(((bf16[6144,4,1,64]{0,3,1,2:T(8,128)(2,1)}), bf16[3072,4,1,64]{0,3,1,2:T(8,128)(2,1)}) %reduce-scatter.6.cloned.1.call-update) | async-done | bytes 1572880 | tf_op jit(solution)/shard_map/reduce_scatter | solution.py:58
  532.1 41.6 %all_to_all.11 = bf16[3072,4,64]{0,2,1:T(8,128)(2,1)S(1)} all-to-all(bf16[3072,4,64]{0,2,1:T(8,128)(2,1)} %bitcast.56), channel_id=1, replica_groups=mesh['expert'=4,'etp'=2,'tp'=4] {'expert'}, dimensions={1} | all-to-all | bytes 3145728 | tf_op jit(solution)/shard_map/all_to_all | solution.py:59
  573.7 1.3 fusion.25
  575.0 0.0 reduce-scatter.8.cloned.1.call-start
  575.1 26.8 %all-gather.7.cloned.1.call-done = bf16[512,3072]{1,0:T(8,128)(2,1)} async-done(((bf16[128,3072]{1,0:T(8,128)(2,1)}), bf16[512,3072]{1,0:T(8,128)(2,1)}) %all-gather.7.cloned.1.call-update) | async-done | bytes 3145744 | tf_op jit(solution)/shard_map/all_gather | solution.py:69
  601.9 10.3 %convolution_convert_fusion.1 = bf16[512,1536]{1,0:T(8,128)(2,1)} fusion(bf16[512,3072]{1,0:T(8,128)(2,1)} %all-gather.7.cloned.1.call-done, bf16[1536,3072]{1,0:T(8,128)(2,1)} %param.17), kind=kOutput, calls=%fused_computation.29 | convolution fusion | flops 4832624640 | bytes 14155776 | tf_op jit(solution)/shard_map/dot_general | solution.py:68
  612.2 26.2 %reduce-scatter.8.cloned.1.call-done = bf16[256,1536]{1,0:T(8,128)(2,1)} async-done(((bf16[512,1536]{1,0:T(8,128)(2,1)}), bf16[256,1536]{1,0:T(8,128)(2,1)}) %reduce-scatter.8.cloned.1.call-update) | async-done | bytes 786448 | tf_op jit(solution)/shard_map/reduce_scatter | solution.py:74
  (17 shorter events, 0.1 us)
Async XLA Ops:
  7.2 93.9 %all-gather.9.cloned.1.call-start = ((), (), s32[]{:S(2)}) async-start(), calls=%async_computation.10 | async-start | bytes 7864320 | tf_op jit(solution)/shard_map/all_gather | solution.py:30
  9.0 280.7 %copy-start.3 = (pred[128,4]{0,1:T(4,128)(4,1)}, pred[128,4]{0,1:T(4,128)(4,1)S(1)}, u32[]{:S(2)}) copy-start(pred[128,4]{0,1:T(4,128)(4,1)S(1)} %copy.12) | copy-start | bytes 1540
  9.6 280.1 %copy-start.1 = (s32[128,4]{0,1:T(4,128)}, s32[128,4]{0,1:T(4,128)S(1)}, u32[]{:S(2)}) copy-start(s32[128,4]{0,1:T(4,128)S(1)} %copy.11) | copy-start | bytes 6148
  55.4 199.8 %all-gather.5.cloned.1.call-start = ((), (), s32[]{:S(2)}) async-start(), calls=%async_computation.5 | async-start | bytes 18874368 | tf_op jit(solution)/shard_map/all_gather | solution.py:33
  101.1 385.6 %reduce-scatter.4.cloned.1.call-start = ((), (), s32[]{:S(2)}) async-start(), calls=%async_computation.6 | async-start | bytes 15728640 | tf_op jit(solution)/shard_map/reduce_scatter | solution.py:55
  255.1 34.6 %copy-start.5 = (bf16[1,1024,2048]{2,1,0:T(8,128)(2,1)S(1)}, bf16[1,1024,2048]{2,1,0:T(8,128)(2,1)}, u32[]{:S(2)}) copy-start(bf16[1,1024,2048]{2,1,0:T(8,128)(2,1)} %param.12) | copy-start | bytes 12582916
  387.4 186.3 %copy-start = (bf16[128,3072]{1,0:T(8,128)(2,1)S(1)}, bf16[128,3072]{1,0:T(8,128)(2,1)}, u32[]{:S(2)}) copy-start(bf16[128,3072]{1,0:T(8,128)(2,1)} %param.9) | copy-start | bytes 2359300
  387.4 186.3 %copy-start.2 = (s32[128,4]{0,1:T(4,128)S(1)}, s32[128,4]{0,1:T(4,128)}, u32[]{:S(2)}) copy-start(s32[128,4]{0,1:T(4,128)} %copy-done.1) | copy-start | bytes 6148
  387.4 186.3 %copy-start.4 = (pred[128,4]{0,1:T(4,128)(4,1)S(1)}, pred[128,4]{0,1:T(4,128)(4,1)}, u32[]{:S(2)}) copy-start(pred[128,4]{0,1:T(4,128)(4,1)} %copy-done.3) | copy-start | bytes 1540
  387.5 144.7 %reduce-scatter.6.cloned.1.call-start = ((), (), s32[]{:S(2)}) async-start(), calls=%async_computation.7 | async-start | bytes 4718592 | tf_op jit(solution)/shard_map/reduce_scatter | solution.py:58
  486.7 115.2 %all-gather.7.cloned.1.call-start = ((), (), s32[]{:S(2)}) async-start(), calls=%async_computation.8 | async-start | bytes 3932160 | tf_op jit(solution)/shard_map/all_gather | solution.py:69
  575.0 63.4 %reduce-scatter.8.cloned.1.call-start = ((), (), s32[]{:S(2)}) async-start(), calls=%async_computation.9 | async-start | bytes 2359296 | tf_op jit(solution)/shard_map/reduce_scatter | solution.py:74
Sparse Core Ops, SparseCore 0:
  55.5 45.5 all-gather.8
  102.6 152.4 all-gather.4
  387.6 99.0 reduce-scatter.3
  488.8 43.3 reduce-scatter.5
  575.2 26.6 all-gather.6
  612.4 26.0 reduce-scatter.7
where the time goes:
time: 646 us; the launch traced here: 645 us
  waiting for transfers between devices  397 us (61%)
  matrix products  136 us (21%)
  blocking collectives  84.7 us (13%)
  between operations  14.2 us (2%)
  local copies, waits for them, and re-layouts  12.6 us (2%)
    all_gather x1, waiting for transfers between devices, body(): shard_piece = lax.all_gather(blocks_all, 'etp', axis=3, tiled=True)  154 us
    reduce_scatter x1, waiting for transfers between devices, body(): lax.psum_scatter(whole_term.astype(jnp.bfloat16), 'tp', scatter_dimension...  99.1 us
    dot_general x1, matrix products, body(): lax.dot_general(gate_local, grad_gate, (((1,), (1,)), ((), ())), preferre...  51.5 us
    all_gather x1, waiting for transfers between devices, body(): blocks_all = lax.all_gather(received[:, None], 'tp', axis=1, tiled=True)  45.6 us
    reduce_scatter x1, waiting for transfers between devices, body(): lax.psum_scatter(by_block, 'etp', scatter_dimension=0, tiled=True)  45.4 us
    all_to_all x1, blocking collectives, body(): lax.all_to_all(outgoing, 'expert', split_axis=0, concat_axis=0, tiled=True)  43.2 us
    all_to_all x1, blocking collectives, body(): lax.all_to_all(reduced.reshape(feat_local, expert_count, cap_slots).astyp...  41.6 us
    dot_general x1, matrix products, body(): lax.dot_general(up_local, grad_up, (((1,), (1,)), ((), ())), preferred_el...  35.3 us
  transfers between devices with their start and end apart: 6, of which 6 were waited for; matrix products, arithmetic and copies ran while one was open for 0% of the time, Pallas kernels for 0%

commit v1 on v0

--- a/solution.py
+++ b/solution.py
@@ -1,10 +1,216 @@
+import functools
+
 import jax
 import jax.numpy as jnp
 from jax import lax
+from jax.experimental import pallas as pl
+from jax.experimental.pallas import tpu as pltpu
 from jax.sharding import PartitionSpec as P
 
-
-def body(d_out, expert_ids, gate_weights, saved_gate, saved_up, w_gate, w_up, w_down, w_out):
+NT = (((1,), (1,)), ((), ()))
+TILE = 256
+COLUMN_PARTS = 4
+
+
+def act_kernel(cap, width, aliased, s_ref, *refs):
+    own0, own1, own2, own3, oth0, oth1, lo2, hi2, lo3, hi3, wd, sg, su = refs[:13]
+    gg, gu, lhs = refs[-3:]
+
+    @pl.when(pl.program_id(0) == 0)
+    def _():
+        mine = pl.ds(pl.multiple_of(s_ref[0], 128), width)
+        other = pl.ds(pl.multiple_of(s_ref[1], 128), width)
+        for r, block in enumerate((own0, own1, own2, own3)):
+            lhs[r * cap:(r + 1) * cap, mine] = block[...]
+        for r, block in enumerate((oth0, oth1)):
+            lhs[r * cap:(r + 1) * cap, other] = block[...]
+        half = cap // 2
+        for r, (low, high) in ((2, (lo2, hi2)), (3, (lo3, hi3))):
+            lhs[r * cap:r * cap + half, other] = low[...]
+            lhs[r * cap + half:(r + 1) * cap, other] = high[...]
+
+    acc = lax.dot_general(lhs[...], wd[...], NT, preferred_element_type=jnp.float32)
+    for r in range(4):
+        rows = pl.ds(pl.multiple_of(s_ref[3 + r], cap), cap)
+        here = slice(r * cap, (r + 1) * cap)
+        g = sg[rows, :].astype(jnp.float32)
+        u = su[rows, :].astype(jnp.float32)
+        s = 1.0 / (1.0 + jnp.exp(-g))
+        d = acc[here, :] * s
+        gu[here, :] = (d * g).astype(jnp.bfloat16)
+        gg[here, :] = (d * u * (1.0 + g * (1.0 - s))).astype(jnp.bfloat16)
+
+
+def act_call(k, scalars, blocks, w_down, saved_gate, saved_up, sofar):
+    cap, width = blocks[0].shape
+    rows_all, hidden = saved_gate.shape[1:]
+    model = w_down.shape[2]
+    rows = 4 * cap
+    full = [pl.BlockSpec(b.shape, lambda n, s: (0, 0)) for b in blocks]
+    wide = pl.BlockSpec((None, TILE, model), lambda n, s: (0, n, 0))
+    saved = pl.BlockSpec((None, rows, TILE), lambda n, s: (0, s[2], n))
+    held = [pl.BlockSpec(memory_space=pl.ANY)] * len(sofar)
+    out = pl.BlockSpec((rows, TILE), lambda n, s: (k, n))
+    count = 1 + len(blocks) + 3
+    return pl.pallas_call(
+        functools.partial(act_kernel, cap, width, len(sofar)),
+        out_shape=[jax.ShapeDtypeStruct((rows_all, hidden), jnp.bfloat16)] * 2,
+        grid_spec=pltpu.PrefetchScalarGridSpec(
+            num_scalar_prefetch=1,
+            grid=(hidden // TILE,),
+            in_specs=full + [wide, saved, saved] + held,
+            out_specs=[out, out],
+            scratch_shapes=[pltpu.VMEM((rows, model), jnp.bfloat16)],
+        ),
+        input_output_aliases={count + i: i for i in range(len(sofar))},
+        compiler_params=pltpu.CompilerParams(vmem_limit_bytes=50 * 2**20),
+        cost_estimate=pl.CostEstimate(
+            flops=2 * rows * model * hidden,
+            bytes_accessed=2 * (hidden * model + rows * model + 4 * rows * hidden),
+            transcendentals=rows * hidden,
+        ),
+        name="act",
+    )(scalars, *blocks, w_down, saved_gate, saved_up, *sofar)
+
+
+def grad_kernel(cap, experts, s_ref, gg, gu, wg, wu, keep, send):
+    res = lax.dot_general(gg[...], wg[...], NT, preferred_element_type=jnp.float32)
+    res += lax.dot_general(gu[...], wu[...], NT, preferred_element_type=jnp.float32)
+    res = res.astype(jnp.bfloat16)
+    for k in range(experts):
+        for v in range(2):
+            at = (4 * k + 2 * v) * cap
+            keep[v, k * cap:(k + 1) * cap, :] = res[at:at + cap]
+            send[v, k * cap:(k + 1) * cap, :] = res[at + cap:at + 2 * cap]
+
+
+def grad_call(part, columns, starts, gg, gu, w_gate, w_up, cap):
+    rows_all, hidden = gg.shape
+    experts = rows_all // (4 * cap)
+    lhs = pl.BlockSpec((rows_all, hidden), lambda h, n, s: (0, 0))
+    first = part * (columns // TILE)
+    wide = pl.BlockSpec((None, TILE, hidden), lambda h, n, s: (0, s[h] + first + n, 0))
+    out = pl.BlockSpec((None, 2, experts * cap, TILE), lambda h, n, s: (h, 0, 0, n))
+    return pl.pallas_call(
+        functools.partial(grad_kernel, cap, experts),
+        out_shape=[jax.ShapeDtypeStruct((2, 2, experts * cap, columns), jnp.bfloat16)] * 2,
+        grid_spec=pltpu.PrefetchScalarGridSpec(
+            num_scalar_prefetch=1,
+            grid=(2, columns // TILE),
+            in_specs=[lhs, lhs, wide, wide],
+            out_specs=[out, out],
+        ),
+        compiler_params=pltpu.CompilerParams(vmem_limit_bytes=50 * 2**20),
+        cost_estimate=pl.CostEstimate(
+            flops=8 * rows_all * hidden * columns,
+            bytes_accessed=2 * (2 * rows_all * hidden + 4 * hidden * columns + 2 * rows_all * columns),
+            transcendentals=0,
+        ),
+        name="grad",
+    )(starts, gg, gu, w_gate, w_up)
+
+
+def planned(d_out, expert_ids, gate_weights, saved_gate, saved_up, w_gate, w_up, w_down, w_out):
+    f32, bf16 = jnp.float32, jnp.bfloat16
+    experts = lax.axis_size("expert")
+    z, x, t = lax.axis_index("expert"), lax.axis_index("etp"), lax.axis_index("tp")
+    y, c = t // 2, t % 2
+    tokens, width = d_out.shape
+    cap = saved_gate.shape[1] // (experts * 4)
+
+    def over_z(v, shift):
+        if shift % experts == 0:
+            return v
+        return lax.ppermute(v, "expert", [(i, (i + shift) % experts) for i in range(experts)])
+
+    def over_x(v):
+        return lax.ppermute(v, "etp", [(0, 1), (1, 0)])
+
+    def over_y(v):
+        return lax.ppermute(v, "tp", [(i, i ^ 2) for i in range(4)])
+
+    def over_core(v):
+        return lax.ppermute(v, "tp", [(i, i ^ 1) for i in range(4)])
+
+    names = (z + jnp.arange(experts, dtype=jnp.int32)) % experts
+    first_hit = expert_ids[:, 0:1] == names[None, :]
+    second_hit = expert_ids[:, 1:2] == names[None, :]
+    member = first_hit.astype(jnp.int32) + second_hit.astype(jnp.int32)
+    weight = gate_weights[:, 0:1] * first_hit.astype(f32) + gate_weights[:, 1:2] * second_hit.astype(f32)
+    slot = jnp.cumsum(member, axis=0) - member
+    slot_iota = jnp.arange(cap, dtype=jnp.int32)
+    select = (slot[:, :, None] == slot_iota[None, None, :]) & (member[:, :, None] > 0)
+    slot_weight = jnp.sum(jnp.where(select, weight[:, :, None], 0.0), axis=0)
+    select = select.astype(bf16)
+
+    gathered = []
+    for k in range(experts):
+        rows = lax.dot_general(
+            select[:, k], d_out, (((0,), (0,)), ((), ())), preferred_element_type=f32
+        )
+        gathered.append(over_z((rows * slot_weight[k][:, None]).astype(bf16), k))
+
+    grads = ()
+    half = cap // 2
+    for k in range(experts):
+        a = gathered[k]
+        bx, by = over_x(a), over_y(a)
+        low, high = over_y(bx[:half]), over_x(by[half:])
+        blocks = (
+            a, over_core(a), by, over_core(by),
+            bx, over_core(bx), low, high, over_core(low), over_core(high),
+        )
+        scalars = jnp.stack(
+            [x * width, (1 - x) * width, (z - k) % experts] + [(t ^ r) * cap for r in range(4)]
+        ).astype(jnp.int32)
+        grads = act_call(k, scalars, blocks, w_down, saved_gate, saved_up, grads)
+    gg, gu = grads
+
+    columns = width // COLUMN_PARTS
+    starts = jnp.stack([x, 1 - x]).astype(jnp.int32) * (width // TILE)
+    cut = experts // 2 * cap
+    hidden_parts, head_rows = [], []
+    for part in range(COLUMN_PARTS):
+        keep, send = grad_call(part, columns, starts, gg, gu, w_gate, w_up, cap)
+        both = (keep.astype(f32) + over_core(send).astype(f32)).astype(bf16)
+        via_x, via_y = over_x(both[1, 1, :cut]), over_y(both[1, 1, cut:])
+        to_y = jnp.concatenate(
+            [(both[0, 1, :cut].astype(f32) + via_x.astype(f32)).astype(bf16), both[0, 1, cut:]]
+        )
+        to_x = jnp.concatenate(
+            [both[1, 0, :cut], (both[1, 0, cut:].astype(f32) + via_y.astype(f32)).astype(bf16)]
+        )
+        from_x, from_y = over_x(to_x), over_y(to_y)
+        own = (both[0, 0].astype(f32) + from_x.astype(f32) + from_y.astype(f32)).astype(bf16)
+        back = [over_z(own[k * cap:(k + 1) * cap], -k) for k in range(experts)]
+        d_moe = 0.0
+        for k in range(experts):
+            d_moe = d_moe + jnp.dot(select[:, k], back[k], preferred_element_type=f32)
+        here = d_out[:, part * columns:(part + 1) * columns].astype(f32)
+        piece = (here + d_moe).astype(bf16)
+        hidden_parts.append(piece)
+        across = over_y(piece)
+        head_rows.append(
+            jnp.concatenate([piece, over_core(piece), across, over_core(across)], axis=0)
+        )
+    d_hidden = jnp.concatenate(hidden_parts, axis=1)
+    head = 0.0
+    for part in range(COLUMN_PARTS):
+        head = head + lax.dot_general(
+            head_rows[part],
+            w_out[:, part * columns:(part + 1) * columns],
+            NT,
+            preferred_element_type=f32,
+        )
+    head = head.astype(bf16).reshape(2, 2 * tokens, w_out.shape[0])
+    mine = jnp.where(y == x, head[0], head[1])
+    theirs = jnp.where(y == x, head[1], head[0])
+    total = (mine.astype(f32) + over_x(theirs).astype(f32)).astype(bf16)
+    swapped = jnp.concatenate([total[tokens:], total[:tokens]], axis=0)
+    return d_hidden, jnp.where(c == 0, total, swapped)
+
+
+def general(d_out, expert_ids, gate_weights, saved_gate, saved_up, w_gate, w_up, w_down, w_out):
     expert_count = lax.axis_size("expert")
     tp_count = lax.axis_size("tp")
     feat_local = d_out.shape[1]
@@ -78,6 +284,8 @@
 
 
 def solution(mesh):
+    pair_of_pairs = mesh.shape["etp"] == 2 and mesh.shape["tp"] == 4
+    body = planned if pair_of_pairs else general
     in_specs = (
         P(("expert", "tp"), "etp"),
         P(("expert", "tp"), None),

time: 646 us -> 365 us (0.57)
  waiting for transfers between devices: 397 us -> 85.2 us
  Pallas kernels: 0 us -> 140 us
  matrix products: 136 us -> 12.3 us
  starting transfers between devices: 0.24 us -> 97 us
  blocking collectives: 84.7 us -> 0 us
  between operations: 14.2 us -> 1.61 us
  other arithmetic: 0.65 us -> 10.1 us
    all_gather x3 -> x0, waiting for transfers between devices: 226 us -> none  [the longest x1 154 us: body(): shard_piece = lax.all_gather(blocks_all, 'etp', axis=3, tiled=True)]
    reduce_scatter x3 -> x0, waiting for transfers between devices: 171 us -> none  [the longest x1 99.1 us: body(): lax.psum_scatter(whole_term.astype(jnp.bfloat16), 'tp', scatter_dimension...]
    pallas_call x0 -> x8, Pallas kernels: none -> 140 us  [the longest x4 77.2 us: grad_call(): pl.pallas_call(functools.partial(grad_kernel, cap, experts), out_shape=[j...]
    dot_general x6 -> x24, matrix products: 136 us -> 12.3 us  [the longest x4 5.9 us: planned(): lax.dot_general(head_rows[part], w_out[:, part * columns:(part + 1) * col...]
    ppermute x0 -> x84, starting transfers between devices: none -> 97 us  [the longest x15 49.6 us: over_z(): lax.ppermute(v, 'expert', [(i, (i + shift) % experts) for i in range(expe...]
    ppermute x0 -> x84, waiting for transfers between devices: none -> 85.2 us  [the longest x17 51.3 us: over_x(): return lax.ppermute(v, 'etp', [(0, 1), (1, 0)])]
    all_to_all x2 -> x0, blocking collectives: 84.7 us -> none  [the longest x1 43.2 us: body(): lax.all_to_all(outgoing, 'expert', split_axis=0, concat_axis=0, tiled=True)]
    unnamed x12 -> x58, local copies, waits for them, and re-layouts: 0.02 us -> 13.2 us
  transfers between devices with their start and end apart: 6 -> 84, of which waited for: 6 -> 20; matrix products, arithmetic and copies ran while one was open for 0% -> 5% of each run, Pallas kernels for 0% -> 23%
where the time goes in v1:
time: 365 us; the launch traced here: 364 us
  Pallas kernels  140 us (38%)
  starting transfers between devices  97 us (27%)
  waiting for transfers between devices  85.2 us (23%)
  local copies, waits for them, and re-layouts  18.5 us (5%)
  matrix products  12.3 us (3%)
  other arithmetic  10.1 us (3%)
    pallas_call x4, Pallas kernels, grad_call(): pl.pallas_call(functools.partial(grad_kernel, cap, experts), out_shape=[j...  77.2 us
    pallas_call x4, Pallas kernels, act_call(): pl.pallas_call(functools.partial(act_kernel, cap, width, len(sofar)), out...  62.5 us
    ppermute x17, waiting for transfers between devices, over_x(): return lax.ppermute(v, 'etp', [(0, 1), (1, 0)])  51.3 us
    ppermute x15, starting transfers between devices, over_z(): lax.ppermute(v, 'expert', [(i, (i + shift) % experts) for i in range(expe...  49.6 us
    ppermute x20, starting transfers between devices, over_y(): return lax.ppermute(v, 'tp', [(i, i ^ 2) for i in range(4)])  22.7 us
    ppermute x20, waiting for transfers between devices, over_y(): return lax.ppermute(v, 'tp', [(i, i ^ 2) for i in range(4)])  22.2 us
    ppermute x17, starting transfers between devices, over_x(): return lax.ppermute(v, 'etp', [(0, 1), (1, 0)])  18.2 us
    unnamed x58, local copies, waits for them, and re-layouts  13.2 us
  transfers between devices with their start and end apart: 84, of which 20 were waited for; matrix products, arithmetic and copies ran while one was open for 5% of the time, Pallas kernels for 23%

profile of v1, /device:TPU:0, one launch (start us, length us, event | category | flops | bytes accessed | tf_op | source)
XLA Modules:
  0.0 364.4 jit_solution(13827277777546243415)
XLA Ops:
  4.7 3.0 collective-permute-start.33
  11.3 2.7 collective-permute-start.10
  14.3 2.5 collective-permute-done.33.refs_4_
  16.8 3.9 %collective-permute-start = (bf16[64,3072]{1,0:T(8,128)(2,1)S(1)}, bf16[64,3072]{1,0:T(8,128)(2,1)}, u32[]{:S(2)}, u32[]{:S(2)}) collective-permute-start(bf16[64,3072]{1,0:T(8,128)(2,1)S(1)} %fusion), channel_id=1, source_target_pairs={{0,24},{8,0},{16,8},{24,16},{1,25},{9,1},{17,9},{25,17},{2,26},{10... | collective-permute-start | bytes 1179656 | tf_op jit(solution)/shard_map/ppermute | solution.py:124
  29.9 10.0 %collective-permute-done.10.refs_0_ = bf16[64,3072]{1,0:T(8,128)(2,1)S(1)} collective-permute-done((bf16[64,3072]{1,0:T(8,128)(2,1)S(1)}, bf16[64,3072]{1,0:T(8,128)(2,1)S(1)}, u32[]{:S(2)}, u32[]{:S(2)}) %collective-permute-start.10) | collective-permute-done | bytes 393248 | tf_op jit(solution)/shard_map/ppermute | solution.py:124
  46.1 5.8 %collective-permute-done.24.refs_4_ = bf16[64,3072]{1,0:T(8,128)(2,1)S(1)} collective-permute-done((bf16[64,3072]{1,0:T(8,128)(2,1)S(1)}, bf16[64,3072]{1,0:T(8,128)(2,1)S(1)}, u32[]{:S(2)}, u32[]{:S(2)}) %collective-permute-start.24) | collective-permute-done | bytes 393248 | tf_op jit(solution)/shard_map/ppermute | solution.py:127
  52.4 6.9 %collective-permute-done.14.refs_4_ = bf16[64,3072]{1,0:T(8,128)(2,1)S(1)} collective-permute-done((bf16[64,3072]{1,0:T(8,128)(2,1)S(1)}, bf16[64,3072]{1,0:T(8,128)(2,1)S(1)}, u32[]{:S(2)}, u32[]{:S(2)}) %collective-permute-start.14) | collective-permute-done | bytes 393248 | tf_op jit(solution)/shard_map/ppermute | solution.py:127
  68.9 2.7 collective-permute-done.4.refs_4_
  72.7 3.7 %collective-permute-done.26.refs_6_ = bf16[32,3072]{1,0:T(8,128)(2,1)} collective-permute-done((bf16[32,3072]{1,0:T(8,128)(2,1)}, bf16[32,3072]{1,0:T(8,128)(2,1)}, u32[]{:S(2)}, u32[]{:S(2)}) %collective-permute-start.26) | collective-permute-done | bytes 196640 | tf_op jit(solution)/shard_map/ppermute | solution.py:130
  76.9 3.6 collective-permute-done.16.refs_6_
  87.8 15.7 %act.4 = (bf16[1024,2048]{1,0:T(8,128)(2,1)}, bf16[1024,2048]{1,0:T(8,128)(2,1)}) custom-call(s32[7]{0:T(128)S(1)} %stack.85.s_ref, bf16[64,3072]{1,0:T(8,128)(2,1)S(1)} %fusion.3.refs_0_, bf16[64,3072]{1,0:T(8,128)(2,1)S(1)} %copy-done.5, bf16[64,3072]{1,0:T(8,128)(2,1)S(1)} %collective-permute-done.31.refs_2_, bf16[64,3072]{1,0:T(8,128)(2,1)S(1)} %copy-done.11, ...), custom_call_target="tpu_custom_call" | custom-call | flops 6442450944 | bytes 32505856 | tf_op jit(solution)/shard_map/act/pallas_call | solution.py:55
  106.1 15.6 %act.5 = (bf16[1024,2048]{1,0:T(8,128)(2,1)}, bf16[1024,2048]{1,0:T(8,128)(2,1)}) custom-call(s32[7]{0:T(128)S(1)} %stack.83.s_ref, bf16[64,3072]{1,0:T(8,128)(2,1)S(1)} %copy-done.3, bf16[64,3072]{1,0:T(8,128)(2,1)S(1)} %copy-done.9, bf16[64,3072]{1,0:T(8,128)(2,1)S(1)} %collective-permute-done.22.refs_2_, ...), custom_call_target="tpu_custom_call", output_to_operand_aliasing={{0}: (14, {}), {1}: (15, {})} | custom-call | flops 6442450944 | bytes 32505856 | tf_op jit(solution)/shard_map/act/pallas_call | solution.py:55
  122.9 15.6 %act.6 = (bf16[1024,2048]{1,0:T(8,128)(2,1)}, bf16[1024,2048]{1,0:T(8,128)(2,1)}) custom-call(s32[7]{0:T(128)S(1)} %stack.81.s_ref, bf16[64,3072]{1,0:T(8,128)(2,1)S(1)} %copy-done.1, bf16[64,3072]{1,0:T(8,128)(2,1)S(1)} %copy-done.7, bf16[64,3072]{1,0:T(8,128)(2,1)S(1)} %collective-permute-done.12.refs_2_, ...), custom_call_target="tpu_custom_call", output_to_operand_aliasing={{0}: (14, {}), {1}: (15, {})} | custom-call | flops 6442450944 | bytes 32505856 | tf_op jit(solution)/shard_map/act/pallas_call | solution.py:55
  138.5 15.6 %act.7 = (bf16[1024,2048]{1,0:T(8,128)(2,1)}, bf16[1024,2048]{1,0:T(8,128)(2,1)}) custom-call(s32[7]{0:T(128)S(1)} %stack.79.s_ref, bf16[64,3072]{1,0:T(8,128)(2,1)} %collective-permute-done.refs_0_, bf16[64,3072]{1,0:T(8,128)(2,1)S(1)} %collective-permute-done.1.refs_1_, ...), custom_call_target="tpu_custom_call", output_to_operand_aliasing={{0}: (14, {}), {1}: (15, {})} | custom-call | flops 6442450944 | bytes 32505856 | tf_op jit(solution)/shard_map/act/pallas_call | solution.py:55
  154.1 19.3 %grad.5 = (bf16[2,2,256,768]{3,2,1,0:T(8,128)(2,1)S(1)}, bf16[2,2,256,768]{3,2,1,0:T(8,128)(2,1)S(1)}) custom-call(s32[2]{0:T(128)S(1)} %add_multiply_fusion.s_ref, bf16[1024,2048]{1,0:T(8,128)(2,1)} %get-tuple-element.24.gg, bf16[1024,2048]{1,0:T(8,128)(2,1)} %get-tuple-element.25.gu, bf16[1,6144,2048]{2,1,0:T(8,128)(2,1)} %wg.7, bf16[1,6144,2048]{2,1,0:T(8,128)(2,1)} %wu.7), custom_call_target="tpu_custom_call" | custom-call | flops 12884901888 | bytes 24117248 | tf_op jit(solution)/shard_map/grad/pallas_call | solution.py:94
  173.4 19.3 %grad.6 = (bf16[2,2,256,768]{3,2,1,0:T(8,128)(2,1)S(1)}, bf16[2,2,256,768]{3,2,1,0:T(8,128)(2,1)S(1)}) custom-call(s32[2]{0:T(128)S(1)} %add_multiply_fusion.s_ref, bf16[1024,2048]{1,0:T(8,128)(2,1)} %get-tuple-element.24.gg, bf16[1024,2048]{1,0:T(8,128)(2,1)} %get-tuple-element.25.gu, bf16[1,6144,2048]{2,1,0:T(8,128)(2,1)} %wg.7, bf16[1,6144,2048]{2,1,0:T(8,128)(2,1)} %wu.7), custom_call_target="tpu_custom_call" | custom-call | flops 12884901888 | bytes 24117248 | tf_op jit(solution)/shard_map/grad/pallas_call | solution.py:94
  193.2 19.3 %grad.7 = (bf16[2,2,256,768]{3,2,1,0:T(8,128)(2,1)S(1)}, bf16[2,2,256,768]{3,2,1,0:T(8,128)(2,1)S(1)}) custom-call(s32[2]{0:T(128)S(1)} %add_multiply_fusion.s_ref, bf16[1024,2048]{1,0:T(8,128)(2,1)} %get-tuple-element.24.gg, bf16[1024,2048]{1,0:T(8,128)(2,1)} %get-tuple-element.25.gu, bf16[1,6144,2048]{2,1,0:T(8,128)(2,1)} %wg.7, bf16[1,6144,2048]{2,1,0:T(8,128)(2,1)} %wu.7), custom_call_target="tpu_custom_call" | custom-call | flops 12884901888 | bytes 24117248 | tf_op jit(solution)/shard_map/grad/pallas_call | solution.py:94
  213.0 19.4 %grad.4 = (bf16[2,2,256,768]{3,2,1,0:T(8,128)(2,1)S(1)}, bf16[2,2,256,768]{3,2,1,0:T(8,128)(2,1)S(1)}) custom-call(s32[2]{0:T(128)S(1)} %add_multiply_fusion.s_ref, bf16[1024,2048]{1,0:T(8,128)(2,1)} %get-tuple-element.24.gg, bf16[1024,2048]{1,0:T(8,128)(2,1)} %get-tuple-element.25.gu, bf16[1,6144,2048]{2,1,0:T(8,128)(2,1)} %wg.7, bf16[1,6144,2048]{2,1,0:T(8,128)(2,1)} %wu.7), custom_call_target="tpu_custom_call" | custom-call | flops 12884901888 | bytes 24117248 | tf_op jit(solution)/shard_map/grad/pallas_call | solution.py:94
  244.5 2.0 collective-permute-done.56
  252.8 2.1 collective-permute-done.40
  257.1 6.7 %collective-permute-done.49 = bf16[256,768]{1,0:T(8,128)(2,1)S(1)} collective-permute-done((bf16[256,768]{1,0:T(8,128)(2,1)S(1)}, bf16[256,768]{1,0:T(8,128)(2,1)S(1)}, u32[]{:S(2)}, u32[]{:S(2)}) %collective-permute-start.49) | collective-permute-done | bytes 393248 | tf_op jit(solution)/shard_map/ppermute | solution.py:127
  266.1 6.1 %collective-permute-done.57 = bf16[256,768]{1,0:T(8,128)(2,1)S(1)} collective-permute-done((bf16[256,768]{1,0:T(8,128)(2,1)S(1)}, bf16[256,768]{1,0:T(8,128)(2,1)S(1)}, u32[]{:S(2)}, u32[]{:S(2)}) %collective-permute-start.57) | collective-permute-done | bytes 393248 | tf_op jit(solution)/shard_map/ppermute | solution.py:127
  273.9 9.4 %collective-permute-start.52 = (bf16[64,768]{1,0:T(8,128)(2,1)S(1)}, bf16[64,768]{1,0:T(8,128)(2,1)S(1)}, u32[]{:S(2)}, u32[]{:S(2)}) collective-permute-start(bf16[64,768]{1,0:T(8,128)(2,1)S(1)} %get-tuple-element.65), channel_id=1, source_target_pairs={{0,24},{8,0},{16,8},{24,16},{1,25},{9,1},{17,9},{25,17},{2,26},{10... | collective-permute-start | bytes 294920 | tf_op jit(solution)/shard_map/ppermute | solution.py:124
  283.4 5.9 %collective-permute-start.54 = (bf16[64,768]{1,0:T(8,128)(2,1)S(1)}, bf16[64,768]{1,0:T(8,128)(2,1)S(1)}, u32[]{:S(2)}, u32[]{:S(2)}) collective-permute-start(bf16[64,768]{1,0:T(8,128)(2,1)S(1)} %get-tuple-element.64), channel_id=1, source_target_pairs={{0,8},{8,16},{16,24},{24,0},{1,9},{9,17},{17,25},{25,1},{2,10},{10... | collective-permute-start | bytes 294920 | tf_op jit(solution)/shard_map/ppermute | solution.py:124
  290.8 6.9 %collective-permute-start.60 = (bf16[64,768]{1,0:T(8,128)(2,1)S(1)}, bf16[64,768]{1,0:T(8,128)(2,1)S(1)}, u32[]{:S(2)}, u32[]{:S(2)}) collective-permute-start(bf16[64,768]{1,0:T(8,128)(2,1)S(1)} %get-tuple-element.68), channel_id=1, source_target_pairs={{0,24},{8,0},{16,8},{24,16},{1,25},{9,1},{17,9},{25,17},{2,26},{10... | collective-permute-start | bytes 294920 | tf_op jit(solution)/shard_map/ppermute | solution.py:124
  299.2 3.3 collective-permute-start.68
  303.7 2.6 collective-permute-start.69
  309.0 8.8 %collective-permute-start.46 = (bf16[64,768]{1,0:T(8,128)(2,1)S(1)}, bf16[64,768]{1,0:T(8,128)(2,1)S(1)}, u32[]{:S(2)}, u32[]{:S(2)}) collective-permute-start(bf16[64,768]{1,0:T(8,128)(2,1)S(1)} %get-tuple-element.61), channel_id=1, source_target_pairs={{0,8},{8,16},{16,24},{24,0},{1,9},{9,17},{17,25},{25,1},{2,10},{10... | collective-permute-start | bytes 294920 | tf_op jit(solution)/shard_map/ppermute | solution.py:124
  326.5 2.6 collective-permute-done.78
  329.1 2.4 collective-permute-start.72
  333.6 3.6 collective-permute-done.72
  342.8 19.1 %collective-permute-done.83 = bf16[256,1536]{1,0:T(8,128)(2,1)} collective-permute-done((bf16[256,1536]{1,0:T(8,128)(2,1)S(1)}, bf16[256,1536]{1,0:T(8,128)(2,1)}, u32[]{:S(2)}, u32[]{:S(2)}) %collective-permute-start.83) | collective-permute-done | bytes 786464 | tf_op jit(solution)/shard_map/ppermute | solution.py:127
  (287 shorter events, 96.9 us)
Async XLA Ops:
  9.5 19.9 %collective-permute-start.20 = (bf16[64,3072]{1,0:T(8,128)(2,1)S(1)}, bf16[64,3072]{1,0:T(8,128)(2,1)S(1)}, u32[]{:S(2)}, u32[]{:S(2)}) collective-permute-start(bf16[64,3072]{1,0:T(8,128)(2,1)S(1)} %fusion.2), channel_id=1, source_target_pairs={{0,8},{8,16},{16,24},{24,0},{1,9},{9,17},{17,25},{25,1},{2,10},{10... | collective-permute-start | bytes 1179656 | tf_op jit(solution)/shard_map/ppermute | solution.py:124
  11.3 28.5 %collective-permute-start.10 = (bf16[64,3072]{1,0:T(8,128)(2,1)S(1)}, bf16[64,3072]{1,0:T(8,128)(2,1)S(1)}, u32[]{:S(2)}, u32[]{:S(2)}) collective-permute-start(bf16[64,3072]{1,0:T(8,128)(2,1)S(1)} %fusion.1), channel_id=1, source_target_pairs={{0,16},{8,24},{16,0},{24,8},{1,17},{9,25},{17,1},{25,9},{2,18},{10... | collective-permute-start | bytes 1179656 | tf_op jit(solution)/shard_map/ppermute | solution.py:124
  16.8 23.6 %collective-permute-start = (bf16[64,3072]{1,0:T(8,128)(2,1)S(1)}, bf16[64,3072]{1,0:T(8,128)(2,1)}, u32[]{:S(2)}, u32[]{:S(2)}) collective-permute-start(bf16[64,3072]{1,0:T(8,128)(2,1)S(1)} %fusion), channel_id=1, source_target_pairs={{0,24},{8,0},{16,8},{24,16},{1,25},{9,1},{17,9},{25,17},{2,26},{10... | collective-permute-start | bytes 1179656 | tf_op jit(solution)/shard_map/ppermute | solution.py:124
  41.6 17.7 %collective-permute-start.14 = (bf16[64,3072]{1,0:T(8,128)(2,1)S(1)}, bf16[64,3072]{1,0:T(8,128)(2,1)S(1)}, u32[]{:S(2)}, u32[]{:S(2)}) collective-permute-start(bf16[64,3072]{1,0:T(8,128)(2,1)S(1)} %collective-permute-done.10.refs_0_), channel_id=1, source_target_pairs={{0,4},{4,0},{1,5},{5,1},{2,6},{6,2},{3,7},{7,3},{8,12},{12,8},{9,1... | collective-permute-start | bytes 1179656 | tf_op jit(solution)/shard_map/ppermute | solution.py:127
  46.1 17.0 %collective-permute-start.34 = (bf16[64,3072]{1,0:T(8,128)(2,1)S(1)}, bf16[64,3072]{1,0:T(8,128)(2,1)S(1)}, u32[]{:S(2)}, u32[]{:S(2)}) collective-permute-start(bf16[64,3072]{1,0:T(8,128)(2,1)S(1)} %collective-permute-done.33.refs_4_), channel_id=1, source_target_pairs={{0,1},{1,0},{2,3},{3,2},{4,5},{5,4},{6,7},{7,6},{8,9},{9,8},{10,11... | collective-permute-start | bytes 1179656 | tf_op jit(solution)/shard_map/ppermute | solution.py:133
  72.1 31.3 %collective-permute-start.6 = (bf16[32,3072]{1,0:T(8,128)(2,1)S(1)}, bf16[32,3072]{1,0:T(8,128)(2,1)S(1)}, u32[]{:S(2)}, u32[]{:S(2)}) collective-permute-start(bf16[32,3072]{1,0:T(8,128)(2,1)S(1)} %slice.338), channel_id=1, source_target_pairs={{0,2},{1,3},{2,0},{3,1},{4,6},{5,7},{6,4},{7,5},{8,10},{9,11},{10,... | collective-permute-start | bytes 589832 | tf_op jit(solution)/shard_map/ppermute | solution.py:130
  76.4 29.1 %collective-permute-start.23 = (bf16[64,3072]{1,0:T(8,128)(2,1)S(1)}, bf16[64,3072]{1,0:T(8,128)(2,1)S(1)}, u32[]{:S(2)}, u32[]{:S(2)}) collective-permute-start(bf16[64,3072]{1,0:T(8,128)(2,1)S(1)} %collective-permute-done.22.refs_2_), channel_id=1, source_target_pairs={{0,1},{1,0},{2,3},{3,2},{4,5},{5,4},{6,7},{7,6},{8,9},{9,8},{10,11... | collective-permute-start | bytes 1179656 | tf_op jit(solution)/shard_map/ppermute | solution.py:133
  76.4 29.2 %collective-permute-start.25 = (bf16[64,3072]{1,0:T(8,128)(2,1)S(1)}, bf16[64,3072]{1,0:T(8,128)(2,1)S(1)}, u32[]{:S(2)}, u32[]{:S(2)}) collective-permute-start(bf16[64,3072]{1,0:T(8,128)(2,1)S(1)} %collective-permute-done.24.refs_4_), channel_id=1, source_target_pairs={{0,1},{1,0},{2,3},{3,2},{4,5},{5,4},{6,7},{7,6},{8,9},{9,8},{10,11... | collective-permute-start | bytes 1179656 | tf_op jit(solution)/shard_map/ppermute | solution.py:133
  80.5 24.5 %collective-permute-start.28 = (bf16[32,3072]{1,0:T(8,128)(2,1)}, bf16[32,3072]{1,0:T(8,128)(2,1)S(1)}, u32[]{:S(2)}, u32[]{:S(2)}) collective-permute-start(bf16[32,3072]{1,0:T(8,128)(2,1)} %collective-permute-done.26.refs_6_), channel_id=1, source_target_pairs={{0,1},{1,0},{2,3},{3,2},{4,5},{5,4},{6,7},{7,6},{8,9},{9,8},{10,11... | collective-permute-start | bytes 589832 | tf_op jit(solution)/shard_map/ppermute | solution.py:133
  80.5 24.5 %collective-permute-start.29 = (bf16[32,3072]{1,0:T(8,128)(2,1)}, bf16[32,3072]{1,0:T(8,128)(2,1)S(1)}, u32[]{:S(2)}, u32[]{:S(2)}) collective-permute-start(bf16[32,3072]{1,0:T(8,128)(2,1)} %collective-permute-done.27.refs_7_), channel_id=1, source_target_pairs={{0,1},{1,0},{2,3},{3,2},{4,5},{5,4},{6,7},{7,6},{8,9},{9,8},{10,11... | collective-permute-start | bytes 589832 | tf_op jit(solution)/shard_map/ppermute | solution.py:133
  103.4 18.2 %collective-permute-start.7 = (bf16[32,3072]{1,0:T(8,128)(2,1)S(1)}, bf16[32,3072]{1,0:T(8,128)(2,1)S(1)}, u32[]{:S(2)}, u32[]{:S(2)}) collective-permute-start(bf16[32,3072]{1,0:T(8,128)(2,1)S(1)} %slice.339), channel_id=1, source_target_pairs={{0,4},{4,0},{1,5},{5,1},{2,6},{6,2},{3,7},{7,3},{8,12},{12,8},{9,1... | collective-permute-start | bytes 589832 | tf_op jit(solution)/shard_map/ppermute | solution.py:127
  105.0 17.3 %collective-permute-start.13 = (bf16[64,3072]{1,0:T(8,128)(2,1)S(1)}, bf16[64,3072]{1,0:T(8,128)(2,1)S(1)}, u32[]{:S(2)}, u32[]{:S(2)}) collective-permute-start(bf16[64,3072]{1,0:T(8,128)(2,1)S(1)} %collective-permute-done.12.refs_2_), channel_id=1, source_target_pairs={{0,1},{1,0},{2,3},{3,2},{4,5},{5,4},{6,7},{7,6},{8,9},{9,8},{10,11... | collective-permute-start | bytes 1179656 | tf_op jit(solution)/shard_map/ppermute | solution.py:133
  105.0 17.8 %collective-permute-start.15 = (bf16[64,3072]{1,0:T(8,128)(2,1)S(1)}, bf16[64,3072]{1,0:T(8,128)(2,1)S(1)}, u32[]{:S(2)}, u32[]{:S(2)}) collective-permute-start(bf16[64,3072]{1,0:T(8,128)(2,1)S(1)} %collective-permute-done.14.refs_4_), channel_id=1, source_target_pairs={{0,1},{1,0},{2,3},{3,2},{4,5},{5,4},{6,7},{7,6},{8,9},{9,8},{10,11... | collective-permute-start | bytes 1179656 | tf_op jit(solution)/shard_map/ppermute | solution.py:133
  105.5 16.3 %collective-permute-start.18 = (bf16[32,3072]{1,0:T(8,128)(2,1)}, bf16[32,3072]{1,0:T(8,128)(2,1)S(1)}, u32[]{:S(2)}, u32[]{:S(2)}) collective-permute-start(bf16[32,3072]{1,0:T(8,128)(2,1)} %collective-permute-done.16.refs_6_), channel_id=1, source_target_pairs={{0,1},{1,0},{2,3},{3,2},{4,5},{5,4},{6,7},{7,6},{8,9},{9,8},{10,11... | collective-permute-start | bytes 589832 | tf_op jit(solution)/shard_map/ppermute | solution.py:133
  105.6 16.7 %collective-permute-start.19 = (bf16[32,3072]{1,0:T(8,128)(2,1)}, bf16[32,3072]{1,0:T(8,128)(2,1)S(1)}, u32[]{:S(2)}, u32[]{:S(2)}) collective-permute-start(bf16[32,3072]{1,0:T(8,128)(2,1)} %collective-permute-done.17.refs_7_), channel_id=1, source_target_pairs={{0,1},{1,0},{2,3},{3,2},{4,5},{5,4},{6,7},{7,6},{8,9},{9,8},{10,11... | collective-permute-start | bytes 589832 | tf_op jit(solution)/shard_map/ppermute | solution.py:133
  121.7 16.8 %collective-permute-start.1 = (bf16[64,3072]{1,0:T(8,128)(2,1)}, bf16[64,3072]{1,0:T(8,128)(2,1)S(1)}, u32[]{:S(2)}, u32[]{:S(2)}) collective-permute-start(bf16[64,3072]{1,0:T(8,128)(2,1)} %collective-permute-done.refs_0_), channel_id=1, source_target_pairs={{0,1},{1,0},{2,3},{3,2},{4,5},{5,4},{6,7},{7,6},{8,9},{9,8},{10,11... | collective-permute-start | bytes 1179656 | tf_op jit(solution)/shard_map/ppermute | solution.py:133
  121.8 16.7 %collective-permute-start.3 = (bf16[64,3072]{1,0:T(8,128)(2,1)S(1)}, bf16[64,3072]{1,0:T(8,128)(2,1)S(1)}, u32[]{:S(2)}, u32[]{:S(2)}) collective-permute-start(bf16[64,3072]{1,0:T(8,128)(2,1)S(1)} %collective-permute-done.2.refs_2_), channel_id=1, source_target_pairs={{0,1},{1,0},{2,3},{3,2},{4,5},{5,4},{6,7},{7,6},{8,9},{9,8},{10,11... | collective-permute-start | bytes 1179656 | tf_op jit(solution)/shard_map/ppermute | solution.py:133
  122.3 16.2 %collective-permute-start.5 = (bf16[64,3072]{1,0:T(8,128)(2,1)S(1)}, bf16[64,3072]{1,0:T(8,128)(2,1)S(1)}, u32[]{:S(2)}, u32[]{:S(2)}) collective-permute-start(bf16[64,3072]{1,0:T(8,128)(2,1)S(1)} %collective-permute-done.4.refs_4_), channel_id=1, source_target_pairs={{0,1},{1,0},{2,3},{3,2},{4,5},{5,4},{6,7},{7,6},{8,9},{9,8},{10,11... | collective-permute-start | bytes 1179656 | tf_op jit(solution)/shard_map/ppermute | solution.py:133
  192.7 40.0 %collective-permute-start.47 = (bf16[2,2,256,768]{3,2,1,0:T(8,128)(2,1)S(1)}, bf16[2,2,256,768]{3,2,1,0:T(8,128)(2,1)}, u32[]{:S(2)}, u32[]{:S(2)}) collective-permute-start(bf16[2,2,256,768]{3,2,1,0:T(8,128)(2,1)S(1)} %get-tuple-element.29), channel_id=1, source_target_pairs={{0,1},{1,0},{2,3},{3,2},{4,5},{5,4},{6,7},{7,6},{8,9},{9,8},{10,11... | collective-permute-start | bytes 4718600 | tf_op jit(solution)/shard_map/ppermute | solution.py:133
  212.4 23.2 %collective-permute-start.55 = (bf16[2,2,256,768]{3,2,1,0:T(8,128)(2,1)S(1)}, bf16[2,2,256,768]{3,2,1,0:T(8,128)(2,1)}, u32[]{:S(2)}, u32[]{:S(2)}) collective-permute-start(bf16[2,2,256,768]{3,2,1,0:T(8,128)(2,1)S(1)} %get-tuple-element.31), channel_id=1, source_target_pairs={{0,1},{1,0},{2,3},{3,2},{4,5},{5,4},{6,7},{7,6},{8,9},{9,8},{10,11... | collective-permute-start | bytes 4718600 | tf_op jit(solution)/shard_map/ppermute | solution.py:133
  212.6 26.5 %collective-permute-start.63 = (bf16[2,2,256,768]{3,2,1,0:T(8,128)(2,1)S(1)}, bf16[2,2,256,768]{3,2,1,0:T(8,128)(2,1)S(1)}, u32[]{:S(2)}, u32[]{:S(2)}) collective-permute-start(bf16[2,2,256,768]{3,2,1,0:T(8,128)(2,1)S(1)} %get-tuple-element.33), channel_id=1, source_target_pairs={{0,1},{1,0},{2,3},{3,2},{4,5},{5,4},{6,7},{7,6},{8,9},{9,8},{10,11... | collective-permute-start | bytes 4718600 | tf_op jit(solution)/shard_map/ppermute | solution.py:133
  247.1 16.7 %collective-permute-start.49 = (bf16[256,768]{1,0:T(8,128)(2,1)S(1)}, bf16[256,768]{1,0:T(8,128)(2,1)S(1)}, u32[]{:S(2)}, u32[]{:S(2)}) collective-permute-start(bf16[256,768]{1,0:T(8,128)(2,1)S(1)} %pad_maximum_fusion.3), channel_id=1, source_target_pairs={{0,4},{4,0},{1,5},{5,1},{2,6},{6,2},{3,7},{7,3},{8,12},{12,8},{9,1... | collective-permute-start | bytes 1179656 | tf_op jit(solution)/shard_map/ppermute | solution.py:127
  251.2 21.0 %collective-permute-start.57 = (bf16[256,768]{1,0:T(8,128)(2,1)S(1)}, bf16[256,768]{1,0:T(8,128)(2,1)S(1)}, u32[]{:S(2)}, u32[]{:S(2)}) collective-permute-start(bf16[256,768]{1,0:T(8,128)(2,1)S(1)} %pad_maximum_fusion.5), channel_id=1, source_target_pairs={{0,4},{4,0},{1,5},{5,1},{2,6},{6,2},{3,7},{7,3},{8,12},{12,8},{9,1... | collective-permute-start | bytes 1179656 | tf_op jit(solution)/shard_map/ppermute | solution.py:127
  254.9 18.9 %collective-permute-start.59 = (bf16[256,768]{1,0:T(8,128)(2,1)S(1)}, bf16[256,768]{1,0:T(8,128)(2,1)S(1)}, u32[]{:S(2)}, u32[]{:S(2)}) collective-permute-start(bf16[256,768]{1,0:T(8,128)(2,1)S(1)} %pad_maximum_fusion.6), channel_id=1, source_target_pairs={{0,2},{1,3},{2,0},{3,1},{4,6},{5,7},{6,4},{7,5},{8,10},{9,11},{10,... | collective-permute-start | bytes 1179656 | tf_op jit(solution)/shard_map/ppermute | solution.py:130
  255.4 28.0 %collective-permute-start.65 = (bf16[256,768]{1,0:T(8,128)(2,1)S(1)}, bf16[256,768]{1,0:T(8,128)(2,1)S(1)}, u32[]{:S(2)}, u32[]{:S(2)}) collective-permute-start(bf16[256,768]{1,0:T(8,128)(2,1)S(1)} %pad_maximum_fusion.7), channel_id=1, source_target_pairs={{0,4},{4,0},{1,5},{5,1},{2,6},{6,2},{3,7},{7,3},{8,12},{12,8},{9,1... | collective-permute-start | bytes 1179656 | tf_op jit(solution)/shard_map/ppermute | solution.py:127
  263.8 25.5 %collective-permute-start.67 = (bf16[256,768]{1,0:T(8,128)(2,1)S(1)}, bf16[256,768]{1,0:T(8,128)(2,1)S(1)}, u32[]{:S(2)}, u32[]{:S(2)}) collective-permute-start(bf16[256,768]{1,0:T(8,128)(2,1)S(1)} %pad_maximum_fusion.8), channel_id=1, source_target_pairs={{0,2},{1,3},{2,0},{3,1},{4,6},{5,7},{6,4},{7,5},{8,10},{9,11},{10,... | collective-permute-start | bytes 1179656 | tf_op jit(solution)/shard_map/ppermute | solution.py:130
  265.4 25.4 %collective-permute-start.41 = (bf16[256,768]{1,0:T(8,128)(2,1)S(1)}, bf16[256,768]{1,0:T(8,128)(2,1)S(1)}, u32[]{:S(2)}, u32[]{:S(2)}) collective-permute-start(bf16[256,768]{1,0:T(8,128)(2,1)S(1)} %pad_maximum_fusion.1), channel_id=1, source_target_pairs={{0,4},{4,0},{1,5},{5,1},{2,6},{6,2},{3,7},{7,3},{8,12},{12,8},{9,1... | collective-permute-start | bytes 1179656 | tf_op jit(solution)/shard_map/ppermute | solution.py:127
  272.2 25.6 %collective-permute-start.43 = (bf16[256,768]{1,0:T(8,128)(2,1)S(1)}, bf16[256,768]{1,0:T(8,128)(2,1)S(1)}, u32[]{:S(2)}, u32[]{:S(2)}) collective-permute-start(bf16[256,768]{1,0:T(8,128)(2,1)S(1)} %pad_maximum_fusion.2), channel_id=1, source_target_pairs={{0,2},{1,3},{2,0},{3,1},{4,6},{5,7},{6,4},{7,5},{8,10},{9,11},{10,... | collective-permute-start | bytes 1179656 | tf_op jit(solution)/shard_map/ppermute | solution.py:130
  273.9 24.1 %collective-permute-start.52 = (bf16[64,768]{1,0:T(8,128)(2,1)S(1)}, bf16[64,768]{1,0:T(8,128)(2,1)S(1)}, u32[]{:S(2)}, u32[]{:S(2)}) collective-permute-start(bf16[64,768]{1,0:T(8,128)(2,1)S(1)} %get-tuple-element.65), channel_id=1, source_target_pairs={{0,24},{8,0},{16,8},{24,16},{1,25},{9,1},{17,9},{25,17},{2,26},{10... | collective-permute-start | bytes 294920 | tf_op jit(solution)/shard_map/ppermute | solution.py:124
  298.0 20.1 %collective-permute-start.61 = (bf16[64,768]{1,0:T(8,128)(2,1)S(1)}, bf16[64,768]{1,0:T(8,128)(2,1)S(1)}, u32[]{:S(2)}, u32[]{:S(2)}) collective-permute-start(bf16[64,768]{1,0:T(8,128)(2,1)S(1)} %get-tuple-element.66), channel_id=1, source_target_pairs={{0,16},{8,24},{16,0},{24,8},{1,17},{9,25},{17,1},{25,9},{2,18},{10... | collective-permute-start | bytes 294920 | tf_op jit(solution)/shard_map/ppermute | solution.py:124
  303.7 17.2 %collective-permute-start.69 = (bf16[64,768]{1,0:T(8,128)(2,1)S(1)}, bf16[64,768]{1,0:T(8,128)(2,1)S(1)}, u32[]{:S(2)}, u32[]{:S(2)}) collective-permute-start(bf16[64,768]{1,0:T(8,128)(2,1)S(1)} %get-tuple-element.69), channel_id=1, source_target_pairs={{0,16},{8,24},{16,0},{24,8},{1,17},{9,25},{17,1},{25,9},{2,18},{10... | collective-permute-start | bytes 294920 | tf_op jit(solution)/shard_map/ppermute | solution.py:124
  341.8 20.1 %collective-permute-start.83 = (bf16[256,1536]{1,0:T(8,128)(2,1)S(1)}, bf16[256,1536]{1,0:T(8,128)(2,1)}, u32[]{:S(2)}, u32[]{:S(2)}) collective-permute-start(bf16[256,1536]{1,0:T(8,128)(2,1)S(1)} %broadcast_select_fusion), channel_id=1, source_target_pairs={{0,4},{4,0},{1,5},{5,1},{2,6},{6,2},{3,7},{7,3},{8,12},{12,8},{9,1... | collective-permute-start | bytes 2359304 | tf_op jit(solution)/shard_map/ppermute | solution.py:127
  (81 other events, 966.2 us)

commit v2 on v1

--- a/solution.py
+++ b/solution.py
@@ -12,68 +12,148 @@
 COLUMN_PARTS = 4
 
 
-def act_kernel(cap, width, aliased, s_ref, *refs):
-    own0, own1, own2, own3, oth0, oth1, lo2, hi2, lo3, hi3, wd, sg, su = refs[:13]
+def send_kernel(sel, rows, scale, *refs):
+    out = refs[-1]
+    picked = jnp.dot(sel[...], rows[...], preferred_element_type=jnp.float32)
+    out[...] = (picked * scale[...]).astype(jnp.bfloat16)
+
+
+def send_call(sel, rows, scale, after):
+    whole = pl.BlockSpec(memory_space=pltpu.VMEM)
+    shape = (sel.shape[0], rows.shape[1])
+    return pl.pallas_call(
+        send_kernel,
+        out_shape=jax.ShapeDtypeStruct(shape, jnp.bfloat16),
+        in_specs=[whole] * 3 + [pl.BlockSpec(memory_space=pl.ANY)] * len(after),
+        out_specs=whole,
+        cost_estimate=pl.CostEstimate(
+            flops=2 * sel.shape[0] * rows.size,
+            bytes_accessed=2 * (rows.size + shape[0] * shape[1]),
+            transcendentals=0,
+        ),
+        name="dispatch",
+    )(sel, rows, scale, *after)
+
+
+def act_kernel(cap, width, groups, s_ref, *refs):
+    blocks = refs[:10 * groups]
+    wd = refs[10 * groups]
+    saved = refs[10 * groups + 1:12 * groups + 1]
     gg, gu, lhs = refs[-3:]
 
     @pl.when(pl.program_id(0) == 0)
     def _():
         mine = pl.ds(pl.multiple_of(s_ref[0], 128), width)
         other = pl.ds(pl.multiple_of(s_ref[1], 128), width)
-        for r, block in enumerate((own0, own1, own2, own3)):
-            lhs[r * cap:(r + 1) * cap, mine] = block[...]
-        for r, block in enumerate((oth0, oth1)):
-            lhs[r * cap:(r + 1) * cap, other] = block[...]
         half = cap // 2
-        for r, (low, high) in ((2, (lo2, hi2)), (3, (lo3, hi3))):
-            lhs[r * cap:r * cap + half, other] = low[...]
-            lhs[r * cap + half:(r + 1) * cap, other] = high[...]
+        for j in range(groups):
+            own0, own1, own2, own3, oth0, oth1, lo2, hi2, lo3, hi3 = blocks[10 * j:10 * j + 10]
+            base = 4 * cap * j
+            for r, block in enumerate((own0, own1, own2, own3)):
+                lhs[base + r * cap:base + (r + 1) * cap, mine] = block[...]
+            for r, block in enumerate((oth0, oth1)):
+                lhs[base + r * cap:base + (r + 1) * cap, other] = block[...]
+            for r, (low, high) in ((2, (lo2, hi2)), (3, (lo3, hi3))):
+                lhs[base + r * cap:base + r * cap + half, other] = low[...]
+                lhs[base + r * cap + half:base + (r + 1) * cap, other] = high[...]
 
     acc = lax.dot_general(lhs[...], wd[...], NT, preferred_element_type=jnp.float32)
-    for r in range(4):
-        rows = pl.ds(pl.multiple_of(s_ref[3 + r], cap), cap)
-        here = slice(r * cap, (r + 1) * cap)
-        g = sg[rows, :].astype(jnp.float32)
-        u = su[rows, :].astype(jnp.float32)
-        s = 1.0 / (1.0 + jnp.exp(-g))
-        d = acc[here, :] * s
-        gu[here, :] = (d * g).astype(jnp.bfloat16)
-        gg[here, :] = (d * u * (1.0 + g * (1.0 - s))).astype(jnp.bfloat16)
-
-
-def act_call(k, scalars, blocks, w_down, saved_gate, saved_up, sofar):
-    cap, width = blocks[0].shape
+    for j in range(groups):
+        sg, su = saved[2 * j:2 * j + 2]
+        for r in range(4):
+            rows = pl.ds(pl.multiple_of(s_ref[2 + r], cap), cap)
+            here = slice((4 * j + r) * cap, (4 * j + r + 1) * cap)
+            g = sg[rows, :].astype(jnp.float32)
+            u = su[rows, :].astype(jnp.float32)
+            s = 1.0 / (1.0 + jnp.exp(-g))
+            d = acc[here, :] * s
+            gu[here, :] = (d * g).astype(jnp.bfloat16)
+            gg[here, :] = (d * u * (1.0 + g * (1.0 - s))).astype(jnp.bfloat16)
+
+
+def act_call(at, first, count, scalars, groups, w_down, saved_gate, saved_up, sofar, after):
+    cap, width = groups[0][0].shape
     rows_all, hidden = saved_gate.shape[1:]
     model = w_down.shape[2]
-    rows = 4 * cap
+    rows = 4 * cap * len(groups)
+    blocks = [b for group in groups for b in group]
     full = [pl.BlockSpec(b.shape, lambda n, s: (0, 0)) for b in blocks]
-    wide = pl.BlockSpec((None, TILE, model), lambda n, s: (0, n, 0))
-    saved = pl.BlockSpec((None, rows, TILE), lambda n, s: (0, s[2], n))
-    held = [pl.BlockSpec(memory_space=pl.ANY)] * len(sofar)
-    out = pl.BlockSpec((rows, TILE), lambda n, s: (k, n))
-    count = 1 + len(blocks) + 3
+    wide = pl.BlockSpec((None, TILE, model), lambda n, s: (0, first + n, 0))
+    saved = []
+    for j in range(len(groups)):
+        saved += [pl.BlockSpec((None, 4 * cap, TILE), lambda n, s, j=j: (0, s[6 + j], first + n))] * 2
+    held = [pl.BlockSpec(memory_space=pl.ANY)] * (len(sofar) + len(after))
+    out = pl.BlockSpec((rows, TILE), lambda n, s: (at, first + n))
+    ahead = 1 + len(blocks) + 1 + len(saved)
     return pl.pallas_call(
-        functools.partial(act_kernel, cap, width, len(sofar)),
+        functools.partial(act_kernel, cap, width, len(groups)),
         out_shape=[jax.ShapeDtypeStruct((rows_all, hidden), jnp.bfloat16)] * 2,
         grid_spec=pltpu.PrefetchScalarGridSpec(
             num_scalar_prefetch=1,
-            grid=(hidden // TILE,),
-            in_specs=full + [wide, saved, saved] + held,
+            grid=(count,),
+            in_specs=full + [wide] + saved + held,
             out_specs=[out, out],
             scratch_shapes=[pltpu.VMEM((rows, model), jnp.bfloat16)],
         ),
-        input_output_aliases={count + i: i for i in range(len(sofar))},
+        input_output_aliases={ahead + i: i for i in range(len(sofar))},
         compiler_params=pltpu.CompilerParams(vmem_limit_bytes=50 * 2**20),
         cost_estimate=pl.CostEstimate(
-            flops=2 * rows * model * hidden,
-            bytes_accessed=2 * (hidden * model + rows * model + 4 * rows * hidden),
-            transcendentals=rows * hidden,
+            flops=2 * rows * model * count * TILE,
+            bytes_accessed=2 * (count * TILE * model + rows * model + 4 * rows * count * TILE),
+            transcendentals=rows * count * TILE,
         ),
         name="act",
-    )(scalars, *blocks, w_down, saved_gate, saved_up, *sofar)
-
-
-def grad_kernel(cap, experts, s_ref, gg, gu, wg, wu, keep, send):
+    )(scalars, *blocks, w_down, *([saved_gate, saved_up] * len(groups)), *sofar, *after)
+
+
+def corner_call(bx, by, after):
+    half = bx.shape[0] // 2
+
+    def kernel(bx_ref, by_ref, *refs):
+        low, high = refs[-2:]
+        low[...] = bx_ref[:half]
+        high[...] = by_ref[half:]
+
+    whole = pl.BlockSpec(memory_space=pltpu.VMEM)
+    return pl.pallas_call(
+        kernel,
+        out_shape=[jax.ShapeDtypeStruct((half, bx.shape[1]), bx.dtype)] * 2,
+        in_specs=[whole] * 2 + [pl.BlockSpec(memory_space=pl.ANY)] * len(after),
+        out_specs=[whole] * 2,
+        cost_estimate=pl.CostEstimate(flops=0, bytes_accessed=6 * bx.size, transcendentals=0),
+        name="corner",
+    )(bx, by, *after)
+
+
+def merge_call(keep, received, other, via_x, via_y, after):
+    rows, columns = keep.shape[1:]
+    cut = rows // 2
+
+    def kernel(keep_ref, got_ref, other_ref, vx_ref, vy_ref, *refs):
+        to_x, to_y, own = refs[-3:]
+        f32 = jnp.float32
+        own[...] = (keep_ref[0].astype(f32) + got_ref[0].astype(f32)).astype(own.dtype)
+        far = keep_ref[1].astype(f32) + got_ref[1].astype(f32)
+        to_y[:cut] = (far[:cut] + vx_ref[...].astype(f32)).astype(to_y.dtype)
+        to_y[cut:] = far[cut:].astype(to_y.dtype)
+        to_x[:cut] = other_ref[0, :cut]
+        to_x[cut:] = (other_ref[0, cut:].astype(f32) + vy_ref[...].astype(f32)).astype(to_x.dtype)
+
+    whole = pl.BlockSpec(memory_space=pltpu.VMEM)
+    return pl.pallas_call(
+        kernel,
+        out_shape=[jax.ShapeDtypeStruct((rows, columns), keep.dtype)] * 3,
+        in_specs=[whole] * 5 + [pl.BlockSpec(memory_space=pl.ANY)] * len(after),
+        out_specs=[whole] * 3,
+        cost_estimate=pl.CostEstimate(
+            flops=4 * rows * columns, bytes_accessed=20 * rows * columns, transcendentals=0
+        ),
+        name="merge",
+    )(keep, received, other, via_x, via_y, *after)
+
+
+def grad_kernel(cap, experts, s_ref, gg, gu, wg, wu, *refs):
+    keep, send = refs[-2:]
     res = lax.dot_general(gg[...], wg[...], NT, preferred_element_type=jnp.float32)
     res += lax.dot_general(gu[...], wu[...], NT, preferred_element_type=jnp.float32)
     res = res.astype(jnp.bfloat16)
@@ -84,30 +164,30 @@
             send[v, k * cap:(k + 1) * cap, :] = res[at + cap:at + 2 * cap]
 
 
-def grad_call(part, columns, starts, gg, gu, w_gate, w_up, cap):
+def grad_call(h, part, columns, starts, gg, gu, w_gate, w_up, cap, after):
     rows_all, hidden = gg.shape
     experts = rows_all // (4 * cap)
-    lhs = pl.BlockSpec((rows_all, hidden), lambda h, n, s: (0, 0))
+    lhs = pl.BlockSpec((rows_all, hidden), lambda n, s: (0, 0))
     first = part * (columns // TILE)
-    wide = pl.BlockSpec((None, TILE, hidden), lambda h, n, s: (0, s[h] + first + n, 0))
-    out = pl.BlockSpec((None, 2, experts * cap, TILE), lambda h, n, s: (h, 0, 0, n))
+    wide = pl.BlockSpec((None, TILE, hidden), lambda n, s: (0, s[h] + first + n, 0))
+    out = pl.BlockSpec((2, experts * cap, TILE), lambda n, s: (0, 0, n))
     return pl.pallas_call(
         functools.partial(grad_kernel, cap, experts),
-        out_shape=[jax.ShapeDtypeStruct((2, 2, experts * cap, columns), jnp.bfloat16)] * 2,
+        out_shape=[jax.ShapeDtypeStruct((2, experts * cap, columns), jnp.bfloat16)] * 2,
         grid_spec=pltpu.PrefetchScalarGridSpec(
             num_scalar_prefetch=1,
-            grid=(2, columns // TILE),
-            in_specs=[lhs, lhs, wide, wide],
+            grid=(columns // TILE,),
+            in_specs=[lhs, lhs, wide, wide] + [pl.BlockSpec(memory_space=pl.ANY)] * len(after),
             out_specs=[out, out],
         ),
         compiler_params=pltpu.CompilerParams(vmem_limit_bytes=50 * 2**20),
         cost_estimate=pl.CostEstimate(
-            flops=8 * rows_all * hidden * columns,
-            bytes_accessed=2 * (2 * rows_all * hidden + 4 * hidden * columns + 2 * rows_all * columns),
+            flops=4 * rows_all * hidden * columns,
+            bytes_accessed=2 * (2 * rows_all * hidden + 2 * hidden * columns + rows_all * columns),
             transcendentals=0,
         ),
         name="grad",
-    )(starts, gg, gu, w_gate, w_up)
+    )(starts, gg, gu, w_gate, w_up, *after)
 
 
 def planned(d_out, expert_ids, gate_weights, saved_gate, saved_up, w_gate, w_up, w_down, w_out):
@@ -143,66 +223,130 @@
     slot_weight = jnp.sum(jnp.where(select, weight[:, :, None], 0.0), axis=0)
     select = select.astype(bf16)
 
-    gathered = []
-    for k in range(experts):
-        rows = lax.dot_general(
-            select[:, k], d_out, (((0,), (0,)), ((), ())), preferred_element_type=f32
-        )
-        gathered.append(over_z((rows * slot_weight[k][:, None]).astype(bf16), k))
-
-    grads = ()
-    half = cap // 2
-    for k in range(experts):
-        a = gathered[k]
-        bx, by = over_x(a), over_y(a)
-        low, high = over_y(bx[:half]), over_x(by[half:])
-        blocks = (
+    order = [0, 1] + list(range(experts - 1, 1, -1))
+    arrived, near, groups = {}, {}, {}
+
+    def fetch(k, after):
+        packed = send_call(select[:, k].T, d_out, slot_weight[k][:, None], after)
+        arrived[k] = over_z(packed, k)
+
+    def spread(k):
+        near[k] = over_x(arrived[k]), over_y(arrived[k])
+
+    def finish(k, after):
+        a, (bx, by) = arrived[k], near[k]
+        corner = corner_call(bx, by, after)
+        low, high = over_y(corner[0]), over_x(corner[1])
+        groups[k] = (
             a, over_core(a), by, over_core(by),
             bx, over_core(bx), low, high, over_core(low), over_core(high),
         )
+
+    for i, k in enumerate(order):
+        fetch(k, () if i < 2 else (arrived[order[i - 1]],))
+        spread(k)
+    tiles = saved_gate.shape[2] // TILE
+    grads = ()
+    pairs = [order[i:i + 2] for i in range(0, experts, 2)]
+    for k in pairs[0]:
+        finish(k, ())
+    for at, pair in enumerate(pairs):
         scalars = jnp.stack(
-            [x * width, (1 - x) * width, (z - k) % experts] + [(t ^ r) * cap for r in range(4)]
+            [x * width, (1 - x) * width]
+            + [(t ^ r) * cap for r in range(4)]
+            + [(z - k) % experts for k in pair]
         ).astype(jnp.int32)
-        grads = act_call(k, scalars, blocks, w_down, saved_gate, saved_up, grads)
+        later = pairs[at + 1] if at + 1 < len(pairs) else []
+        cuts = (0, tiles // 2, tiles) if later else (0, tiles)
+        for i in range(len(cuts) - 1):
+            after = ()
+            if later:
+                after = (arrived[later[0]],) if i == 0 else (*near[later[0]], arrived[later[-1]])
+            grads = act_call(
+                at, cuts[i], cuts[i + 1] - cuts[i], scalars, [groups[k] for k in pair],
+                w_down, saved_gate, saved_up, grads, after,
+            )
+            if later and i < len(later):
+                finish(later[i], (grads[0],))
+        for k in later:
+            if k not in groups:
+                finish(k, ())
     gg, gu = grads
 
     columns = width // COLUMN_PARTS
     starts = jnp.stack([x, 1 - x]).astype(jnp.int32) * (width // TILE)
     cut = experts // 2 * cap
-    hidden_parts, head_rows = [], []
+    order = [k % experts for k in order]
+
+    def add(*terms):
+        return sum(v.astype(f32) for v in terms).astype(bf16)
+
+    kept = {}
+    summed, merged, owned, pieces, head_rows = {}, {}, {}, {}, []
+
+    def stage_sum(h, part):
+        keep, sent = kept[h, part]
+        summed[h, part] = add(keep, sent)
+
+    def stage_merge(part, after):
+        merged[part] = merge_call(*kept[0, part], summed[1, part], *steps[part], after)
+
+    def stage_own(part):
+        to_x, to_y, base = merged[part]
+        owned[part] = add(base, over_x(to_x), over_y(to_y))
+
+    def stage_piece(part):
+        own = owned[part]
+        d_moe = 0.0
+        for i, k in enumerate(order):
+            back = over_z(own[i * cap:(i + 1) * cap], -k)
+            d_moe = d_moe + jnp.dot(select[:, k], back, preferred_element_type=f32)
+        here = d_out[:, part * columns:(part + 1) * columns].astype(f32)
+        pieces[part] = (here + d_moe).astype(bf16)
+        across = over_y(pieces[part])
+        both = jnp.concatenate([pieces[part], across], axis=0)
+        head_rows.append((both, over_core(both)))
+
+    steps = {}
     for part in range(COLUMN_PARTS):
-        keep, send = grad_call(part, columns, starts, gg, gu, w_gate, w_up, cap)
-        both = (keep.astype(f32) + over_core(send).astype(f32)).astype(bf16)
-        via_x, via_y = over_x(both[1, 1, :cut]), over_y(both[1, 1, cut:])
-        to_y = jnp.concatenate(
-            [(both[0, 1, :cut].astype(f32) + via_x.astype(f32)).astype(bf16), both[0, 1, cut:]]
-        )
-        to_x = jnp.concatenate(
-            [both[1, 0, :cut], (both[1, 0, cut:].astype(f32) + via_y.astype(f32)).astype(bf16)]
-        )
-        from_x, from_y = over_x(to_x), over_y(to_y)
-        own = (both[0, 0].astype(f32) + from_x.astype(f32) + from_y.astype(f32)).astype(bf16)
-        back = [over_z(own[k * cap:(k + 1) * cap], -k) for k in range(experts)]
-        d_moe = 0.0
-        for k in range(experts):
-            d_moe = d_moe + jnp.dot(select[:, k], back[k], preferred_element_type=f32)
-        here = d_out[:, part * columns:(part + 1) * columns].astype(f32)
-        piece = (here + d_moe).astype(bf16)
-        hidden_parts.append(piece)
-        across = over_y(piece)
-        head_rows.append(
-            jnp.concatenate([piece, over_core(piece), across, over_core(across)], axis=0)
-        )
+        for h in (1, 0):
+            after = []
+            if h == 1:
+                if part >= 1:
+                    stage_sum(1, part - 1)
+                    s1 = summed[1, part - 1]
+                    steps[part - 1] = over_x(s1[1, :cut]), over_y(s1[1, cut:])
+                    after.append(s1)
+                if part >= 2:
+                    stage_own(part - 2)
+                    after.append(owned[part - 2])
+            else:
+                if part >= 1:
+                    stage_merge(part - 1, (kept[1, part][0],))
+                    after += merged[part - 1][:2]
+                if part >= 2:
+                    stage_piece(part - 2)
+                    after.append(pieces[part - 2])
+            keep, sent = grad_call(h, part, columns, starts, gg, gu, w_gate, w_up, cap, after)
+            kept[h, part] = keep, over_core(sent)
+    end = COLUMN_PARTS - 1
+    stage_sum(1, end)
+    s1 = summed[1, end]
+    steps[end] = over_x(s1[1, :cut]), over_y(s1[1, cut:])
+    stage_merge(end, ())
+    for part in range(max(end - 1, 0), COLUMN_PARTS):
+        stage_own(part)
+        stage_piece(part)
+    hidden_parts = [pieces[part] for part in range(COLUMN_PARTS)]
     d_hidden = jnp.concatenate(hidden_parts, axis=1)
-    head = 0.0
-    for part in range(COLUMN_PARTS):
-        head = head + lax.dot_general(
-            head_rows[part],
-            w_out[:, part * columns:(part + 1) * columns],
-            NT,
-            preferred_element_type=f32,
-        )
-    head = head.astype(bf16).reshape(2, 2 * tokens, w_out.shape[0])
+    own_core = jnp.concatenate([rows for rows, _ in head_rows], axis=1)
+    other_core = jnp.concatenate([rows for _, rows in head_rows], axis=1)
+    head = jnp.stack(
+        [
+            lax.dot_general(rows, w_out, NT, preferred_element_type=f32).astype(bf16)
+            for rows in (own_core, other_core)
+        ]
+    ).reshape(2, 2, tokens, w_out.shape[0]).transpose(1, 0, 2, 3).reshape(2, 2 * tokens, -1)
     mine = jnp.where(y == x, head[0], head[1])
     theirs = jnp.where(y == x, head[1], head[0])
     total = (mine.astype(f32) + over_x(theirs).astype(f32)).astype(bf16)

time: 365 us -> 422 us (1.16)
  waiting for transfers between devices: 85.2 us -> 121 us
  starting transfers between devices: 97 us -> 62.5 us
  Pallas kernels: 140 us -> 171 us
  local copies, waits for them, and re-layouts: 18.5 us -> 35.5 us
  matrix products: 12.3 us -> 17 us
    ppermute x15, waiting for transfers between devices: 11.5 us -> 45.6 us  [over_z(): lax.ppermute(v, 'expert', [(i, (i + shift) % experts) for i in range(expe...]
    ppermute x15, starting transfers between devices: 49.6 us -> 18.2 us  [over_z(): lax.ppermute(v, 'expert', [(i, (i + shift) % experts) for i in range(expe...]
    pallas_call x4 -> x8, Pallas kernels: 77.2 us -> 95.5 us  [grad_call(): pl.pallas_call(functools.partial(grad_kernel, cap, experts), out_shape=[j...]
    unnamed x58 -> x154, local copies, waits for them, and re-layouts: 13.2 us -> 29.1 us
    ppermute x20, waiting for transfers between devices: 22.2 us -> 37.9 us  [over_y(): return lax.ppermute(v, 'tp', [(i, i ^ 2) for i in range(4)])]
    ppermute x17, waiting for transfers between devices: 51.3 us -> 35.8 us  [over_x(): return lax.ppermute(v, 'etp', [(0, 1), (1, 0)])]
    pallas_call x4 -> x15, Pallas kernels: 62.5 us -> 75.3 us  [the longest x3 47.6 us: act_call(): pl.pallas_call(functools.partial(act_kernel, cap, width, len(groups)), ou...]
    dot_general x24 -> x18, matrix products: 12.3 us -> 17 us  [the longest x2 10.1 us: planned(): lax.dot_general(rows, w_out, NT, preferred_element_type=f32).astype(bf16)]
  transfers between devices with their start and end apart: 84 -> 84, of which waited for: 20 -> 26; matrix products, arithmetic and copies ran while one was open for 5% -> 5% of each run, Pallas kernels for 23% -> 32%
where the time goes in v2:
time: 422 us; the launch traced here: 418 us
  Pallas kernels  171 us (41%)
  waiting for transfers between devices  121 us (29%)
  starting transfers between devices  62.5 us (15%)
  local copies, waits for them, and re-layouts  35.5 us (8%)
  matrix products  17 us (4%)
  other arithmetic  8.88 us (2%)
    pallas_call x8, Pallas kernels, grad_call(): pl.pallas_call(functools.partial(grad_kernel, cap, experts), out_shape=[j...  95.5 us
    pallas_call x3, Pallas kernels, act_call(): pl.pallas_call(functools.partial(act_kernel, cap, width, len(groups)), ou...  47.6 us
    ppermute x15, waiting for transfers between devices, over_z(): lax.ppermute(v, 'expert', [(i, (i + shift) % experts) for i in range(expe...  45.6 us
    ppermute x20, waiting for transfers between devices, over_y(): return lax.ppermute(v, 'tp', [(i, i ^ 2) for i in range(4)])  37.9 us
    ppermute x17, waiting for transfers between devices, over_x(): return lax.ppermute(v, 'etp', [(0, 1), (1, 0)])  35.8 us
    unnamed x154, local copies, waits for them, and re-layouts  29.1 us
    ppermute x20, starting transfers between devices, over_y(): return lax.ppermute(v, 'tp', [(i, i ^ 2) for i in range(4)])  21.8 us
    ppermute x15, starting transfers between devices, over_z(): lax.ppermute(v, 'expert', [(i, (i + shift) % experts) for i in range(expe...  18.2 us
  transfers between devices with their start and end apart: 84, of which 26 were waited for; matrix products, arithmetic and copies ran while one was open for 5% of the time, Pallas kernels for 32%

profile of v2, /device:TPU:0, one launch (start us, length us, event | category | flops | bytes accessed | tf_op | source)
XLA Modules:
  0.0 417.8 jit_solution(12540539174933419729)
XLA Ops:
  7.4 3.0 collective-permute-start
  16.3 5.6 %collective-permute-done.refs_0_.refs_10_ = bf16[64,3072]{1,0:T(8,128)(2,1)} collective-permute-done((bf16[64,3072]{1,0:T(8,128)(2,1)}, bf16[64,3072]{1,0:T(8,128)(2,1)}, u32[]{:S(2)}, u32[]{:S(2)}) %collective-permute-start) | collective-permute-done | bytes 393248 | tf_op jit(solution)/shard_map/ppermute | solution.py:204
  31.6 6.3 %collective-permute-done.12.refs_6_ = bf16[32,3072]{1,0:T(8,128)(2,1)S(1)} collective-permute-done((bf16[32,3072]{1,0:T(8,128)(2,1)}, bf16[32,3072]{1,0:T(8,128)(2,1)S(1)}, u32[]{:S(2)}, u32[]{:S(2)}) %collective-permute-start.12) | collective-permute-done | bytes 196640 | tf_op jit(solution)/shard_map/ppermute | solution.py:210
  48.3 3.5 collective-permute-done.1.refs_25_.refs_0_
  63.7 11.2 %collective-permute-done.29.refs_29_.refs_10_ = bf16[64,3072]{1,0:T(8,128)(2,1)} collective-permute-done((bf16[64,3072]{1,0:T(8,128)(2,1)}, bf16[64,3072]{1,0:T(8,128)(2,1)}, u32[]{:S(2)}, u32[]{:S(2)}) %collective-permute-start.29) | collective-permute-done | bytes 393248 | tf_op jit(solution)/shard_map/ppermute | solution.py:204
  84.0 13.3 %act.3 = (bf16[1024,2048]{1,0:T(8,128)(2,1)}, bf16[1024,2048]{1,0:T(8,128)(2,1)}) custom-call(s32[8]{0:T(128)S(1)} %stack.74.s_ref, bf16[64,3072]{1,0:T(8,128)(2,1)S(1)} %copy-done.13, bf16[64,3072]{1,0:T(8,128)(2,1)S(1)} %collective-permute-done.7.refs_1_, bf16[64,3072]{1,0:T(8,128)(2,1)S(1)} %copy-done.10, ...), custom_call_target="tpu_custom_call" | custom-call | flops 6442450944 | bytes 23068672 | tf_op jit(solution)/shard_map/act/pallas_call | solution.py:88
  101.7 4.5 %collective-permute-done.25.refs_6_ = bf16[32,3072]{1,0:T(8,128)(2,1)} collective-permute-done((bf16[32,3072]{1,0:T(8,128)(2,1)}, bf16[32,3072]{1,0:T(8,128)(2,1)}, u32[]{:S(2)}, u32[]{:S(2)}) %collective-permute-start.25) | collective-permute-done | bytes 196640 | tf_op jit(solution)/shard_map/ppermute | solution.py:210
  113.7 12.8 %act.4 = (bf16[1024,2048]{1,0:T(8,128)(2,1)}, bf16[1024,2048]{1,0:T(8,128)(2,1)}) custom-call(s32[8]{0:T(128)S(1)} %stack.74.s_ref, bf16[64,3072]{1,0:T(8,128)(2,1)S(1)} %copy-done.13, bf16[64,3072]{1,0:T(8,128)(2,1)S(1)} %collective-permute-done.7.refs_1_, bf16[64,3072]{1,0:T(8,128)(2,1)S(1)} %copy-done.10, ...), custom_call_target="tpu_custom_call", output_to_operand_aliasing={{0}: (26, {}), {1}: (27, {})} | custom-call | flops 6442450944 | bytes 23068672 | tf_op jit(solution)/shard_map/act/pallas_call | solution.py:88
  132.0 4.0 collective-permute-done.35.refs_16_
  139.6 21.5 %act.5 = (bf16[1024,2048]{1,0:T(8,128)(2,1)}, bf16[1024,2048]{1,0:T(8,128)(2,1)}) custom-call(s32[8]{0:T(128)S(1)} %stack.71.s_ref, bf16[64,3072]{1,0:T(8,128)(2,1)S(1)} %copy-done.12, bf16[64,3072]{1,0:T(8,128)(2,1)} %collective-permute-done.2.refs_1_, bf16[64,3072]{1,0:T(8,128)(2,1)S(1)} %copy-done.4, ...), custom_call_target="tpu_custom_call", output_to_operand_aliasing={{0}: (26, {}), {1}: (27, {})} | custom-call | flops 12884901888 | bytes 39845888 | tf_op jit(solution)/shard_map/act/pallas_call | solution.py:88
  161.1 11.9 %grad.9 = (bf16[2,256,768]{2,1,0:T(8,128)(2,1)S(1)}, bf16[2,256,768]{2,1,0:T(8,128)(2,1)S(1)}) custom-call(s32[2]{0:T(128)S(1)} %add_multiply_fusion.s_ref, bf16[1024,2048]{1,0:T(8,128)(2,1)} %get-tuple-element.56.gg, bf16[1024,2048]{1,0:T(8,128)(2,1)} %get-tuple-element.57.gu, bf16[1,6144,2048]{2,1,0:T(8,128)(2,1)} %wg.15, bf16[1,6144,2048]{2,1,0:T(8,128)(2,1)} %wu.15), custom_call_target="tpu_custom_call" | custom-call | flops 6442450944 | bytes 16252928 | tf_op jit(solution)/shard_map/grad/pallas_call | solution.py:174
  173.2 11.9 %grad.8 = (bf16[2,256,768]{2,1,0:T(8,128)(2,1)S(1)}, bf16[2,256,768]{2,1,0:T(8,128)(2,1)S(1)}) custom-call(s32[2]{0:T(128)S(1)} %add_multiply_fusion.s_ref, bf16[1024,2048]{1,0:T(8,128)(2,1)} %get-tuple-element.56.gg, bf16[1024,2048]{1,0:T(8,128)(2,1)} %get-tuple-element.57.gu, bf16[1,6144,2048]{2,1,0:T(8,128)(2,1)} %wg.15, bf16[1,6144,2048]{2,1,0:T(8,128)(2,1)} %wu.15), custom_call_target="tpu_custom_call" | custom-call | flops 6442450944 | bytes 16252928 | tf_op jit(solution)/shard_map/grad/pallas_call | solution.py:174
  188.3 12.0 %grad.10 = (bf16[2,256,768]{2,1,0:T(8,128)(2,1)S(1)}, bf16[2,256,768]{2,1,0:T(8,128)(2,1)S(1)}) custom-call(s32[2]{0:T(128)S(1)} %add_multiply_fusion.s_ref, bf16[1024,2048]{1,0:T(8,128)(2,1)} %get-tuple-element.56.gg, bf16[1024,2048]{1,0:T(8,128)(2,1)} %get-tuple-element.57.gu, bf16[1,6144,2048]{2,1,0:T(8,128)(2,1)} %wg.15, bf16[1,6144,2048]{2,1,0:T(8,128)(2,1)} %wu.15, ...), custom_call_target="tpu_custom_call" | custom-call | flops 6442450944 | bytes 16252928 | tf_op jit(solution)/shard_map/grad/pallas_call | solution.py:174
  207.6 8.4 %collective-permute-done.43 = bf16[256,768]{1,0:T(8,128)(2,1)S(1)} collective-permute-done((bf16[256,768]{1,0:T(8,128)(2,1)}, bf16[256,768]{1,0:T(8,128)(2,1)S(1)}, u32[]{:S(2)}, u32[]{:S(2)}) %collective-permute-start.43) | collective-permute-done | bytes 393248 | tf_op jit(solution)/shard_map/ppermute | solution.py:207
  217.9 3.9 collective-permute-start.45
  221.8 11.9 %grad.11 = (bf16[2,256,768]{2,1,0:T(8,128)(2,1)S(1)}, bf16[2,256,768]{2,1,0:T(8,128)(2,1)S(1)}) custom-call(s32[2]{0:T(128)S(1)} %add_multiply_fusion.s_ref, bf16[1024,2048]{1,0:T(8,128)(2,1)} %get-tuple-element.56.gg, bf16[1024,2048]{1,0:T(8,128)(2,1)} %get-tuple-element.57.gu, bf16[1,6144,2048]{2,1,0:T(8,128)(2,1)} %wg.15, bf16[1,6144,2048]{2,1,0:T(8,128)(2,1)} %wu.15, ...), custom_call_target="tpu_custom_call" | custom-call | flops 6442450944 | bytes 16252928 | tf_op jit(solution)/shard_map/grad/pallas_call | solution.py:174
  234.7 7.3 %collective-permute-done.47 = bf16[64,768]{1,0:T(8,128)(2,1)S(1)} collective-permute-done((bf16[64,768]{1,0:T(8,128)(2,1)S(1)}, bf16[64,768]{1,0:T(8,128)(2,1)S(1)}, u32[]{:S(2)}, u32[]{:S(2)}) %collective-permute-start.47) | collective-permute-done | bytes 98336 | tf_op jit(solution)/shard_map/ppermute | solution.py:204
  245.2 11.9 %grad.12 = (bf16[2,256,768]{2,1,0:T(8,128)(2,1)S(1)}, bf16[2,256,768]{2,1,0:T(8,128)(2,1)S(1)}) custom-call(s32[2]{0:T(128)S(1)} %add_multiply_fusion.s_ref, bf16[1024,2048]{1,0:T(8,128)(2,1)} %get-tuple-element.56.gg, bf16[1024,2048]{1,0:T(8,128)(2,1)} %get-tuple-element.57.gu, bf16[1,6144,2048]{2,1,0:T(8,128)(2,1)} %wg.15, bf16[1,6144,2048]{2,1,0:T(8,128)(2,1)} %wu.15, ...), custom_call_target="tpu_custom_call" | custom-call | flops 6442450944 | bytes 16252928 | tf_op jit(solution)/shard_map/grad/pallas_call | solution.py:174
  259.1 2.9 merge.5
  266.3 11.0 %collective-permute-done.75 = bf16[128,768]{1,0:T(8,128)(2,1)S(1)} collective-permute-done((bf16[128,768]{1,0:T(8,128)(2,1)S(1)}, bf16[128,768]{1,0:T(8,128)(2,1)S(1)}, u32[]{:S(2)}, u32[]{:S(2)}) %collective-permute-start.75) | collective-permute-done | bytes 196640 | tf_op jit(solution)/shard_map/ppermute | solution.py:210
  278.9 11.9 %grad.13 = (bf16[2,256,768]{2,1,0:T(8,128)(2,1)S(1)}, bf16[2,256,768]{2,1,0:T(8,128)(2,1)S(1)}) custom-call(s32[2]{0:T(128)S(1)} %add_multiply_fusion.s_ref, bf16[1024,2048]{1,0:T(8,128)(2,1)} %get-tuple-element.56.gg, bf16[1024,2048]{1,0:T(8,128)(2,1)} %get-tuple-element.57.gu, bf16[1,6144,2048]{2,1,0:T(8,128)(2,1)} %wg.15, bf16[1,6144,2048]{2,1,0:T(8,128)(2,1)} %wu.15, ...), custom_call_target="tpu_custom_call" | custom-call | flops 6442450944 | bytes 16252928 | tf_op jit(solution)/shard_map/grad/pallas_call | solution.py:174
  293.6 7.6 %collective-permute-done.56 = bf16[64,768]{1,0:T(8,128)(2,1)S(1)} collective-permute-done((bf16[64,768]{1,0:T(8,128)(2,1)S(1)}, bf16[64,768]{1,0:T(8,128)(2,1)S(1)}, u32[]{:S(2)}, u32[]{:S(2)}) %collective-permute-start.56) | collective-permute-done | bytes 98336 | tf_op jit(solution)/shard_map/ppermute | solution.py:204
  303.9 12.1 %grad.14 = (bf16[2,256,768]{2,1,0:T(8,128)(2,1)S(1)}, bf16[2,256,768]{2,1,0:T(8,128)(2,1)S(1)}) custom-call(s32[2]{0:T(128)S(1)} %add_multiply_fusion.s_ref, bf16[1024,2048]{1,0:T(8,128)(2,1)} %get-tuple-element.56.gg, bf16[1024,2048]{1,0:T(8,128)(2,1)} %get-tuple-element.57.gu, bf16[1,6144,2048]{2,1,0:T(8,128)(2,1)} %wg.15, bf16[1,6144,2048]{2,1,0:T(8,128)(2,1)} %wu.15, ...), custom_call_target="tpu_custom_call" | custom-call | flops 6442450944 | bytes 16252928 | tf_op jit(solution)/shard_map/grad/pallas_call | solution.py:174
  325.2 11.9 %grad.15 = (bf16[2,256,768]{2,1,0:T(8,128)(2,1)S(1)}, bf16[2,256,768]{2,1,0:T(8,128)(2,1)S(1)}) custom-call(s32[2]{0:T(128)S(1)} %add_multiply_fusion.s_ref, bf16[1024,2048]{1,0:T(8,128)(2,1)} %get-tuple-element.56.gg, bf16[1024,2048]{1,0:T(8,128)(2,1)} %get-tuple-element.57.gu, bf16[1,6144,2048]{2,1,0:T(8,128)(2,1)} %wg.15, bf16[1,6144,2048]{2,1,0:T(8,128)(2,1)} %wu.15, ...), custom_call_target="tpu_custom_call" | custom-call | flops 6442450944 | bytes 16252928 | tf_op jit(solution)/shard_map/grad/pallas_call | solution.py:174
  341.2 2.9 collective-permute-done.63
  347.8 4.1 collective-permute-done.69.vy_ref
  359.6 5.7 %collective-permute-done.70 = bf16[256,768]{1,0:T(8,128)(2,1)S(1)} collective-permute-done((bf16[256,768]{1,0:T(8,128)(2,1)}, bf16[256,768]{1,0:T(8,128)(2,1)S(1)}, u32[]{:S(2)}, u32[]{:S(2)}) %collective-permute-start.70) | collective-permute-done | bytes 393248 | tf_op jit(solution)/shard_map/ppermute | solution.py:207
  366.3 2.9 collective-permute-start.72
  380.9 4.8 %collective-permute-done.78 = bf16[128,768]{1,0:T(8,128)(2,1)S(1)} collective-permute-done((bf16[128,768]{1,0:T(8,128)(2,1)S(1)}, bf16[128,768]{1,0:T(8,128)(2,1)S(1)}, u32[]{:S(2)}, u32[]{:S(2)}) %collective-permute-start.78) | collective-permute-done | bytes 196640 | tf_op jit(solution)/shard_map/ppermute | solution.py:210
  385.9 6.5 %convolution_convert_fusion.1 = bf16[256,1536]{1,0:T(8,128)(2,1)S(1)} fusion(bf16[1536,3072]{1,0:T(8,128)(2,1)} %param.17, bf16[128,768]{1,0:T(8,128)(2,1)S(1)} %collective-permute-done.78, bf16[128,768]{1,0:T(8,128)(2,1)S(1)} %fusion.34, bf16[128,768]{1,0:T(8,128)(2,1)S(1)} %collective-permute-done.77, bf16[128,768]{1,0:T(8,128)(2,1)S(1)} %fusion.33, ...), kind=kOutput, calls=%fused_computation.1 | convolution fusion | flops 2428895232 | bytes 11796480 | tf_op jit(solution)/shard_map/dot_general | solution.py:346
  392.4 3.6 convolution_convert_fusion
  398.3 17.9 %collective-permute-done.83 = bf16[256,1536]{1,0:T(8,128)(2,1)S(1)} collective-permute-done((bf16[256,1536]{1,0:T(8,128)(2,1)S(1)}, bf16[256,1536]{1,0:T(8,128)(2,1)S(1)}, u32[]{:S(2)}, u32[]{:S(2)}) %collective-permute-start.83) | collective-permute-done | bytes 786464 | tf_op jit(solution)/shard_map/ppermute | solution.py:207
  (380 shorter events, 145.0 us)
Async XLA Ops:
  16.2 23.8 %collective-permute-start.7 = (bf16[64,3072]{1,0:T(8,128)(2,1)}, bf16[64,3072]{1,0:T(8,128)(2,1)S(1)}, u32[]{:S(2)}, u32[]{:S(2)}) collective-permute-start(bf16[64,3072]{1,0:T(8,128)(2,1)} %dispatch.6.refs_0_), channel_id=1, source_target_pairs={{0,1},{1,0},{2,3},{3,2},{4,5},{5,4},{6,7},{7,6},{8,9},{9,8},{10,11... | collective-permute-start | bytes 1179656 | tf_op jit(solution)/shard_map/ppermute | solution.py:213
  21.8 20.8 %collective-permute-start.17 = (bf16[64,3072]{1,0:T(8,128)(2,1)}, bf16[64,3072]{1,0:T(8,128)(2,1)}, u32[]{:S(2)}, u32[]{:S(2)}) collective-permute-start(bf16[64,3072]{1,0:T(8,128)(2,1)} %collective-permute-done.refs_0_.refs_10_), channel_id=1, source_target_pairs={{0,2},{1,3},{2,0},{3,1},{4,6},{5,7},{6,4},{7,5},{8,10},{9,11},{10,... | collective-permute-start | bytes 1179656 | tf_op jit(solution)/shard_map/ppermute | solution.py:210
  23.4 19.6 %collective-permute-start.19 = (bf16[64,3072]{1,0:T(8,128)(2,1)}, bf16[64,3072]{1,0:T(8,128)(2,1)}, u32[]{:S(2)}, u32[]{:S(2)}) collective-permute-start(bf16[64,3072]{1,0:T(8,128)(2,1)} %collective-permute-done.refs_0_.refs_10_), channel_id=1, source_target_pairs={{0,4},{4,0},{1,5},{5,1},{2,6},{6,2},{3,7},{7,3},{8,12},{12,8},{9,1... | collective-permute-start | bytes 1179656 | tf_op jit(solution)/shard_map/ppermute | solution.py:207
  54.7 20.3 %collective-permute-start.29 = (bf16[64,3072]{1,0:T(8,128)(2,1)}, bf16[64,3072]{1,0:T(8,128)(2,1)}, u32[]{:S(2)}, u32[]{:S(2)}) collective-permute-start(bf16[64,3072]{1,0:T(8,128)(2,1)} %dispatch.7), channel_id=1, source_target_pairs={{0,16},{8,24},{16,0},{24,8},{1,17},{9,25},{17,1},{25,9},{2,18},{10... | collective-permute-start | bytes 1179656 | tf_op jit(solution)/shard_map/ppermute | solution.py:204
  57.3 19.2 %collective-permute-start.18 = (bf16[64,3072]{1,0:T(8,128)(2,1)}, bf16[64,3072]{1,0:T(8,128)(2,1)}, u32[]{:S(2)}, u32[]{:S(2)}) collective-permute-start(bf16[64,3072]{1,0:T(8,128)(2,1)} %collective-permute-done.17.by_ref.refs_12_), channel_id=1, source_target_pairs={{0,1},{1,0},{2,3},{3,2},{4,5},{5,4},{6,7},{7,6},{8,9},{9,8},{10,11... | collective-permute-start | bytes 1179656 | tf_op jit(solution)/shard_map/ppermute | solution.py:213
  57.3 20.2 %collective-permute-start.20 = (bf16[64,3072]{1,0:T(8,128)(2,1)}, bf16[64,3072]{1,0:T(8,128)(2,1)}, u32[]{:S(2)}, u32[]{:S(2)}) collective-permute-start(bf16[64,3072]{1,0:T(8,128)(2,1)} %collective-permute-done.19.bx_ref.refs_14_), channel_id=1, source_target_pairs={{0,1},{1,0},{2,3},{3,2},{4,5},{5,4},{6,7},{7,6},{8,9},{9,8},{10,11... | collective-permute-start | bytes 1179656 | tf_op jit(solution)/shard_map/ppermute | solution.py:213
  60.2 37.1 %collective-permute-start.3 = (bf16[64,3072]{1,0:T(8,128)(2,1)}, bf16[64,3072]{1,0:T(8,128)(2,1)S(1)}, u32[]{:S(2)}, u32[]{:S(2)}) collective-permute-start(bf16[64,3072]{1,0:T(8,128)(2,1)} %copy-done.11), channel_id=1, source_target_pairs={{0,2},{1,3},{2,0},{3,1},{4,6},{5,7},{6,4},{7,5},{8,10},{9,11},{10,... | collective-permute-start | bytes 1179656 | tf_op jit(solution)/shard_map/ppermute | solution.py:210
  62.5 34.9 %collective-permute-start.5 = (bf16[64,3072]{1,0:T(8,128)(2,1)}, bf16[64,3072]{1,0:T(8,128)(2,1)S(1)}, u32[]{:S(2)}, u32[]{:S(2)}) collective-permute-start(bf16[64,3072]{1,0:T(8,128)(2,1)} %copy-done.11), channel_id=1, source_target_pairs={{0,4},{4,0},{1,5},{5,1},{2,6},{6,2},{3,7},{7,3},{8,12},{12,8},{9,1... | collective-permute-start | bytes 1179656 | tf_op jit(solution)/shard_map/ppermute | solution.py:207
  75.0 31.6 %collective-permute-start.31 = (bf16[64,3072]{1,0:T(8,128)(2,1)}, bf16[64,3072]{1,0:T(8,128)(2,1)}, u32[]{:S(2)}, u32[]{:S(2)}) collective-permute-start(bf16[64,3072]{1,0:T(8,128)(2,1)} %collective-permute-done.29.refs_29_.refs_10_), channel_id=1, source_target_pairs={{0,2},{1,3},{2,0},{3,1},{4,6},{5,7},{6,4},{7,5},{8,10},{9,11},{10,... | collective-permute-start | bytes 1179656 | tf_op jit(solution)/shard_map/ppermute | solution.py:210
  76.5 30.6 %collective-permute-start.33 = (bf16[64,3072]{1,0:T(8,128)(2,1)}, bf16[64,3072]{1,0:T(8,128)(2,1)}, u32[]{:S(2)}, u32[]{:S(2)}) collective-permute-start(bf16[64,3072]{1,0:T(8,128)(2,1)} %collective-permute-done.29.refs_29_.refs_10_), channel_id=1, source_target_pairs={{0,4},{4,0},{1,5},{5,1},{2,6},{6,2},{3,7},{7,3},{8,12},{12,8},{9,1... | collective-permute-start | bytes 1179656 | tf_op jit(solution)/shard_map/ppermute | solution.py:207
  101.6 26.8 %collective-permute-start.2 = (bf16[64,3072]{1,0:T(8,128)(2,1)S(1)}, bf16[64,3072]{1,0:T(8,128)(2,1)}, u32[]{:S(2)}, u32[]{:S(2)}) collective-permute-start(bf16[64,3072]{1,0:T(8,128)(2,1)S(1)} %copy-done.12), channel_id=1, source_target_pairs={{0,1},{1,0},{2,3},{3,2},{4,5},{5,4},{6,7},{7,6},{8,9},{9,8},{10,11... | collective-permute-start | bytes 1179656 | tf_op jit(solution)/shard_map/ppermute | solution.py:213
  106.1 25.4 %collective-permute-start.30 = (bf16[64,3072]{1,0:T(8,128)(2,1)}, bf16[64,3072]{1,0:T(8,128)(2,1)}, u32[]{:S(2)}, u32[]{:S(2)}) collective-permute-start(bf16[64,3072]{1,0:T(8,128)(2,1)} %collective-permute-done.29.refs_29_.refs_10_), channel_id=1, source_target_pairs={{0,1},{1,0},{2,3},{3,2},{4,5},{5,4},{6,7},{7,6},{8,9},{9,8},{10,11... | collective-permute-start | bytes 1179656 | tf_op jit(solution)/shard_map/ppermute | solution.py:213
  106.6 24.9 %collective-permute-start.4 = (bf16[64,3072]{1,0:T(8,128)(2,1)}, bf16[64,3072]{1,0:T(8,128)(2,1)}, u32[]{:S(2)}, u32[]{:S(2)}) collective-permute-start(bf16[64,3072]{1,0:T(8,128)(2,1)} %copy-done.3), channel_id=1, source_target_pairs={{0,1},{1,0},{2,3},{3,2},{4,5},{5,4},{6,7},{7,6},{8,9},{9,8},{10,11... | collective-permute-start | bytes 1179656 | tf_op jit(solution)/shard_map/ppermute | solution.py:213
  106.6 22.3 %collective-permute-start.27 = (bf16[32,3072]{1,0:T(8,128)(2,1)}, bf16[32,3072]{1,0:T(8,128)(2,1)}, u32[]{:S(2)}, u32[]{:S(2)}) collective-permute-start(bf16[32,3072]{1,0:T(8,128)(2,1)} %collective-permute-done.25.refs_6_), channel_id=1, source_target_pairs={{0,1},{1,0},{2,3},{3,2},{4,5},{5,4},{6,7},{7,6},{8,9},{9,8},{10,11... | collective-permute-start | bytes 589832 | tf_op jit(solution)/shard_map/ppermute | solution.py:213
  107.1 23.4 %collective-permute-start.28 = (bf16[32,3072]{1,0:T(8,128)(2,1)}, bf16[32,3072]{1,0:T(8,128)(2,1)}, u32[]{:S(2)}, u32[]{:S(2)}) collective-permute-start(bf16[32,3072]{1,0:T(8,128)(2,1)} %collective-permute-done.26.refs_7_), channel_id=1, source_target_pairs={{0,1},{1,0},{2,3},{3,2},{4,5},{5,4},{6,7},{7,6},{8,9},{9,8},{10,11... | collective-permute-start | bytes 589832 | tf_op jit(solution)/shard_map/ppermute | solution.py:213
  186.0 15.2 %collective-permute-start.39 = (bf16[2,256,768]{2,1,0:T(8,128)(2,1)S(1)}, bf16[2,256,768]{2,1,0:T(8,128)(2,1)S(1)}, u32[]{:S(2)}, u32[]{:S(2)}) collective-permute-start(bf16[2,256,768]{2,1,0:T(8,128)(2,1)S(1)} %get-tuple-element.59), channel_id=1, source_target_pairs={{0,1},{1,0},{2,3},{3,2},{4,5},{5,4},{6,7},{7,6},{8,9},{9,8},{10,11... | collective-permute-start | bytes 2359304 | tf_op jit(solution)/shard_map/ppermute | solution.py:213
  207.6 35.0 %collective-permute-start.49 = (bf16[2,256,768]{2,1,0:T(8,128)(2,1)S(1)}, bf16[2,256,768]{2,1,0:T(8,128)(2,1)S(1)}, u32[]{:S(2)}, u32[]{:S(2)}) collective-permute-start(bf16[2,256,768]{2,1,0:T(8,128)(2,1)S(1)} %get-tuple-element.68), channel_id=1, source_target_pairs={{0,1},{1,0},{2,3},{3,2},{4,5},{5,4},{6,7},{7,6},{8,9},{9,8},{10,11... | collective-permute-start | bytes 2359304 | tf_op jit(solution)/shard_map/ppermute | solution.py:213
  217.9 16.6 %collective-permute-start.45 = (bf16[64,768]{1,0:T(8,128)(2,1)S(1)}, bf16[64,768]{1,0:T(8,128)(2,1)S(1)}, u32[]{:S(2)}, u32[]{:S(2)}) collective-permute-start(bf16[64,768]{1,0:T(8,128)(2,1)S(1)} %get-tuple-element.109), channel_id=1, source_target_pairs={{0,24},{8,0},{16,8},{24,16},{1,25},{9,1},{17,9},{25,17},{2,26},{10... | collective-permute-start | bytes 294920 | tf_op jit(solution)/shard_map/ppermute | solution.py:204
  233.7 24.4 %collective-permute-start.48 = (bf16[2,256,768]{2,1,0:T(8,128)(2,1)S(1)}, bf16[2,256,768]{2,1,0:T(8,128)(2,1)S(1)}, u32[]{:S(2)}, u32[]{:S(2)}) collective-permute-start(bf16[2,256,768]{2,1,0:T(8,128)(2,1)S(1)} %get-tuple-element.67), channel_id=1, source_target_pairs={{0,1},{1,0},{2,3},{3,2},{4,5},{5,4},{6,7},{7,6},{8,9},{9,8},{10,11... | collective-permute-start | bytes 2359304 | tf_op jit(solution)/shard_map/ppermute | solution.py:213
  233.9 29.8 %collective-permute-start.46 = (bf16[64,768]{1,0:T(8,128)(2,1)S(1)}, bf16[64,768]{1,0:T(8,128)(2,1)}, u32[]{:S(2)}, u32[]{:S(2)}) collective-permute-start(bf16[64,768]{1,0:T(8,128)(2,1)S(1)} %get-tuple-element.107), channel_id=1, source_target_pairs={{0,8},{8,16},{16,24},{24,0},{1,9},{9,17},{17,25},{25,1},{2,10},{10... | collective-permute-start | bytes 294920 | tf_op jit(solution)/shard_map/ppermute | solution.py:204
  242.8 15.2 %collective-permute-start.50 = (bf16[128,768]{1,0:T(8,128)(2,1)S(1)}, bf16[128,768]{1,0:T(8,128)(2,1)S(1)}, u32[]{:S(2)}, u32[]{:S(2)}) collective-permute-start(bf16[128,768]{1,0:T(8,128)(2,1)S(1)} %get-tuple-element.95), channel_id=1, source_target_pairs={{0,4},{4,0},{1,5},{5,1},{2,6},{6,2},{3,7},{7,3},{8,12},{12,8},{9,1... | collective-permute-start | bytes 589832 | tf_op jit(solution)/shard_map/ppermute | solution.py:207
  262.0 15.3 %collective-permute-start.52 = (bf16[256,768]{1,0:T(8,128)(2,1)}, bf16[256,768]{1,0:T(8,128)(2,1)}, u32[]{:S(2)}, u32[]{:S(2)}) collective-permute-start(bf16[256,768]{1,0:T(8,128)(2,1)} %get-tuple-element.71.refs_0_), channel_id=1, source_target_pairs={{0,4},{4,0},{1,5},{5,1},{2,6},{6,2},{3,7},{7,3},{8,12},{12,8},{9,1... | collective-permute-start | bytes 1179656 | tf_op jit(solution)/shard_map/ppermute | solution.py:207
  266.3 35.5 %collective-permute-start.58 = (bf16[2,256,768]{2,1,0:T(8,128)(2,1)S(1)}, bf16[2,256,768]{2,1,0:T(8,128)(2,1)S(1)}, u32[]{:S(2)}, u32[]{:S(2)}) collective-permute-start(bf16[2,256,768]{2,1,0:T(8,128)(2,1)S(1)} %get-tuple-element.75), channel_id=1, source_target_pairs={{0,1},{1,0},{2,3},{3,2},{4,5},{5,4},{6,7},{7,6},{8,9},{9,8},{10,11... | collective-permute-start | bytes 2359304 | tf_op jit(solution)/shard_map/ppermute | solution.py:213
  277.3 115.1 %collective-permute-start.79 = (bf16[256,768]{1,0:T(8,128)(2,1)S(1)}, bf16[256,768]{1,0:T(8,128)(2,1)}, u32[]{:S(2)}, u32[]{:S(2)}) collective-permute-start(bf16[256,768]{1,0:T(8,128)(2,1)S(1)} %pad_maximum_fusion.1), channel_id=1, source_target_pairs={{0,1},{1,0},{2,3},{3,2},{4,5},{5,4},{6,7},{7,6},{8,9},{9,8},{10,11... | collective-permute-start | bytes 1179656 | tf_op jit(solution)/shard_map/ppermute | solution.py:213
  290.8 26.2 %collective-permute-start.57 = (bf16[2,256,768]{2,1,0:T(8,128)(2,1)S(1)}, bf16[2,256,768]{2,1,0:T(8,128)(2,1)S(1)}, u32[]{:S(2)}, u32[]{:S(2)}) collective-permute-start(bf16[2,256,768]{2,1,0:T(8,128)(2,1)S(1)} %get-tuple-element.74), channel_id=1, source_target_pairs={{0,1},{1,0},{2,3},{3,2},{4,5},{5,4},{6,7},{7,6},{8,9},{9,8},{10,11... | collective-permute-start | bytes 2359304 | tf_op jit(solution)/shard_map/ppermute | solution.py:213
  316.9 21.7 %collective-permute-start.67 = (bf16[2,256,768]{2,1,0:T(8,128)(2,1)S(1)}, bf16[2,256,768]{2,1,0:T(8,128)(2,1)}, u32[]{:S(2)}, u32[]{:S(2)}) collective-permute-start(bf16[2,256,768]{2,1,0:T(8,128)(2,1)S(1)} %get-tuple-element.82), channel_id=1, source_target_pairs={{0,1},{1,0},{2,3},{3,2},{4,5},{5,4},{6,7},{7,6},{8,9},{9,8},{10,11... | collective-permute-start | bytes 2359304 | tf_op jit(solution)/shard_map/ppermute | solution.py:213
  320.9 16.3 %collective-permute-start.61 = (bf16[256,768]{1,0:T(8,128)(2,1)}, bf16[256,768]{1,0:T(8,128)(2,1)S(1)}, u32[]{:S(2)}, u32[]{:S(2)}) collective-permute-start(bf16[256,768]{1,0:T(8,128)(2,1)} %get-tuple-element.78.refs_0_), channel_id=1, source_target_pairs={{0,4},{4,0},{1,5},{5,1},{2,6},{6,2},{3,7},{7,3},{8,12},{12,8},{9,1... | collective-permute-start | bytes 1179656 | tf_op jit(solution)/shard_map/ppermute | solution.py:207
  321.8 15.4 %collective-permute-start.62 = (bf16[256,768]{1,0:T(8,128)(2,1)}, bf16[256,768]{1,0:T(8,128)(2,1)S(1)}, u32[]{:S(2)}, u32[]{:S(2)}) collective-permute-start(bf16[256,768]{1,0:T(8,128)(2,1)} %get-tuple-element.79.refs_1_), channel_id=1, source_target_pairs={{0,2},{1,3},{2,0},{3,1},{4,6},{5,7},{6,4},{7,5},{8,10},{9,11},{10,... | collective-permute-start | bytes 1179656 | tf_op jit(solution)/shard_map/ppermute | solution.py:210
  338.7 18.7 %collective-permute-start.65 = (bf16[64,768]{1,0:T(8,128)(2,1)}, bf16[64,768]{1,0:T(8,128)(2,1)}, u32[]{:S(2)}, u32[]{:S(2)}) collective-permute-start(bf16[64,768]{1,0:T(8,128)(2,1)} %get-tuple-element.99), channel_id=1, source_target_pairs={{0,16},{8,24},{16,0},{24,8},{1,17},{9,25},{17,1},{25,9},{2,18},{10... | collective-permute-start | bytes 294920 | tf_op jit(solution)/shard_map/ppermute | solution.py:204
  347.1 32.9 %collective-permute-start.76 = (bf16[128,768]{1,0:T(8,128)(2,1)S(1)}, bf16[128,768]{1,0:T(8,128)(2,1)S(1)}, u32[]{:S(2)}, u32[]{:S(2)}) collective-permute-start(bf16[128,768]{1,0:T(8,128)(2,1)S(1)} %fusion.32.refs_2_), channel_id=1, source_target_pairs={{0,2},{1,3},{2,0},{3,1},{4,6},{5,7},{6,4},{7,5},{8,10},{9,11},{10,... | collective-permute-start | bytes 589832 | tf_op jit(solution)/shard_map/ppermute | solution.py:210
  351.9 17.3 %collective-permute-start.64 = (bf16[64,768]{1,0:T(8,128)(2,1)S(1)}, bf16[64,768]{1,0:T(8,128)(2,1)}, u32[]{:S(2)}, u32[]{:S(2)}) collective-permute-start(bf16[64,768]{1,0:T(8,128)(2,1)S(1)} %get-tuple-element.98), channel_id=1, source_target_pairs={{0,8},{8,16},{16,24},{24,0},{1,9},{9,17},{17,25},{25,1},{2,10},{10... | collective-permute-start | bytes 294920 | tf_op jit(solution)/shard_map/ppermute | solution.py:204
  396.4 19.8 %collective-permute-start.83 = (bf16[256,1536]{1,0:T(8,128)(2,1)S(1)}, bf16[256,1536]{1,0:T(8,128)(2,1)S(1)}, u32[]{:S(2)}, u32[]{:S(2)}) collective-permute-start(bf16[256,1536]{1,0:T(8,128)(2,1)S(1)} %bitcast.108), channel_id=1, source_target_pairs={{0,4},{4,0},{1,5},{5,1},{2,6},{6,2},{3,7},{7,3},{8,12},{12,8},{9,1... | collective-permute-start | bytes 2359304 | tf_op jit(solution)/shard_map/ppermute | solution.py:207
  (129 other events, 916.3 us)

commit v3 on v1

--- a/solution.py
+++ b/solution.py
@@ -12,68 +12,79 @@
 COLUMN_PARTS = 4
 
 
-def act_kernel(cap, width, aliased, s_ref, *refs):
-    own0, own1, own2, own3, oth0, oth1, lo2, hi2, lo3, hi3, wd, sg, su = refs[:13]
+def act_kernel(cap, width, groups, s_ref, *refs):
+    blocks = refs[:10 * groups]
+    wd = refs[10 * groups]
+    saved = refs[10 * groups + 1:12 * groups + 1]
     gg, gu, lhs = refs[-3:]
 
     @pl.when(pl.program_id(0) == 0)
     def _():
         mine = pl.ds(pl.multiple_of(s_ref[0], 128), width)
         other = pl.ds(pl.multiple_of(s_ref[1], 128), width)
-        for r, block in enumerate((own0, own1, own2, own3)):
-            lhs[r * cap:(r + 1) * cap, mine] = block[...]
-        for r, block in enumerate((oth0, oth1)):
-            lhs[r * cap:(r + 1) * cap, other] = block[...]
         half = cap // 2
-        for r, (low, high) in ((2, (lo2, hi2)), (3, (lo3, hi3))):
-            lhs[r * cap:r * cap + half, other] = low[...]
-            lhs[r * cap + half:(r + 1) * cap, other] = high[...]
+        for j in range(groups):
+            own0, own1, own2, own3, oth0, oth1, lo2, hi2, lo3, hi3 = blocks[10 * j:10 * j + 10]
+            base = 4 * cap * j
+            for r, block in enumerate((own0, own1, own2, own3)):
+                lhs[base + r * cap:base + (r + 1) * cap, mine] = block[...]
+            for r, block in enumerate((oth0, oth1)):
+                lhs[base + r * cap:base + (r + 1) * cap, other] = block[...]
+            for r, (low, high) in ((2, (lo2, hi2)), (3, (lo3, hi3))):
+                lhs[base + r * cap:base + r * cap + half, other] = low[...]
+                lhs[base + r * cap + half:base + (r + 1) * cap, other] = high[...]
 
     acc = lax.dot_general(lhs[...], wd[...], NT, preferred_element_type=jnp.float32)
-    for r in range(4):
-        rows = pl.ds(pl.multiple_of(s_ref[3 + r], cap), cap)
-        here = slice(r * cap, (r + 1) * cap)
-        g = sg[rows, :].astype(jnp.float32)
-        u = su[rows, :].astype(jnp.float32)
-        s = 1.0 / (1.0 + jnp.exp(-g))
-        d = acc[here, :] * s
-        gu[here, :] = (d * g).astype(jnp.bfloat16)
-        gg[here, :] = (d * u * (1.0 + g * (1.0 - s))).astype(jnp.bfloat16)
-
-
-def act_call(k, scalars, blocks, w_down, saved_gate, saved_up, sofar):
-    cap, width = blocks[0].shape
+    for j in range(groups):
+        sg, su = saved[2 * j:2 * j + 2]
+        for r in range(4):
+            rows = pl.ds(pl.multiple_of(s_ref[2 + r], cap), cap)
+            here = slice((4 * j + r) * cap, (4 * j + r + 1) * cap)
+            g = sg[rows, :].astype(jnp.float32)
+            u = su[rows, :].astype(jnp.float32)
+            s = 1.0 / (1.0 + jnp.exp(-g))
+            d = acc[here, :] * s
+            gu[here, :] = (d * g).astype(jnp.bfloat16)
+            gg[here, :] = (d * u * (1.0 + g * (1.0 - s))).astype(jnp.bfloat16)
+
+
+def act_call(at, first, count, scalars, groups, w_down, saved_gate, saved_up, sofar, after):
+    cap, width = groups[0][0].shape
     rows_all, hidden = saved_gate.shape[1:]
     model = w_down.shape[2]
-    rows = 4 * cap
+    rows = 4 * cap * len(groups)
+    blocks = [b for group in groups for b in group]
     full = [pl.BlockSpec(b.shape, lambda n, s: (0, 0)) for b in blocks]
-    wide = pl.BlockSpec((None, TILE, model), lambda n, s: (0, n, 0))
-    saved = pl.BlockSpec((None, rows, TILE), lambda n, s: (0, s[2], n))
-    held = [pl.BlockSpec(memory_space=pl.ANY)] * len(sofar)
-    out = pl.BlockSpec((rows, TILE), lambda n, s: (k, n))
-    count = 1 + len(blocks) + 3
+    wide = pl.BlockSpec((None, TILE, model), lambda n, s: (0, first + n, 0))
+    saved = []
+    for j in range(len(groups)):
+        saved += [pl.BlockSpec((None, 4 * cap, TILE), lambda n, s, j=j: (0, s[6 + j], first + n))] * 2
+    held = [pl.BlockSpec(memory_space=pl.ANY)] * (len(sofar) + len(after))
+    out = pl.BlockSpec((rows, TILE), lambda n, s: (at, first + n))
+    ahead = 1 + len(blocks) + 1 + len(saved)
     return pl.pallas_call(
-        functools.partial(act_kernel, cap, width, len(sofar)),
+        functools.partial(act_kernel, cap, width, len(groups)),
         out_shape=[jax.ShapeDtypeStruct((rows_all, hidden), jnp.bfloat16)] * 2,
         grid_spec=pltpu.PrefetchScalarGridSpec(
             num_scalar_prefetch=1,
-            grid=(hidden // TILE,),
-            in_specs=full + [wide, saved, saved] + held,
+            grid=(count,),
+            in_specs=full + [wide] + saved + held,
             out_specs=[out, out],
             scratch_shapes=[pltpu.VMEM((rows, model), jnp.bfloat16)],
         ),
-        input_output_aliases={count + i: i for i in range(len(sofar))},
+        input_output_aliases={ahead + i: i for i in range(len(sofar))},
         compiler_params=pltpu.CompilerParams(vmem_limit_bytes=50 * 2**20),
         cost_estimate=pl.CostEstimate(
-            flops=2 * rows * model * hidden,
-            bytes_accessed=2 * (hidden * model + rows * model + 4 * rows * hidden),
-            transcendentals=rows * hidden,
+            flops=2 * rows * model * count * TILE,
+            bytes_accessed=2 * (count * TILE * model + rows * model + 4 * rows * count * TILE),
+            transcendentals=rows * count * TILE,
         ),
         name="act",
-    )(scalars, *blocks, w_down, saved_gate, saved_up, *sofar)
-
-
-def grad_kernel(cap, experts, s_ref, gg, gu, wg, wu, keep, send):
+    )(scalars, *blocks, w_down, *([saved_gate, saved_up] * len(groups)), *sofar, *after)
+
+
+def grad_kernel(cap, experts, s_ref, gg, gu, wg, wu, *refs):
+    keep, send = refs[-2:]
     res = lax.dot_general(gg[...], wg[...], NT, preferred_element_type=jnp.float32)
     res += lax.dot_general(gu[...], wu[...], NT, preferred_element_type=jnp.float32)
     res = res.astype(jnp.bfloat16)
@@ -84,7 +95,7 @@
             send[v, k * cap:(k + 1) * cap, :] = res[at + cap:at + 2 * cap]
 
 
-def grad_call(part, columns, starts, gg, gu, w_gate, w_up, cap):
+def grad_call(part, columns, starts, gg, gu, w_gate, w_up, cap, after):
     rows_all, hidden = gg.shape
     experts = rows_all // (4 * cap)
     lhs = pl.BlockSpec((rows_all, hidden), lambda h, n, s: (0, 0))
@@ -97,7 +108,7 @@
         grid_spec=pltpu.PrefetchScalarGridSpec(
             num_scalar_prefetch=1,
             grid=(2, columns // TILE),
-            in_specs=[lhs, lhs, wide, wide],
+            in_specs=[lhs, lhs, wide, wide] + [pl.BlockSpec(memory_space=pl.ANY)] * len(after),
             out_specs=[out, out],
         ),
         compiler_params=pltpu.CompilerParams(vmem_limit_bytes=50 * 2**20),
@@ -107,7 +118,7 @@
             transcendentals=0,
         ),
         name="grad",
-    )(starts, gg, gu, w_gate, w_up)
+    )(starts, gg, gu, w_gate, w_up, *after)
 
 
 def planned(d_out, expert_ids, gate_weights, saved_gate, saved_up, w_gate, w_up, w_down, w_out):
@@ -150,29 +161,42 @@
         )
         gathered.append(over_z((rows * slot_weight[k][:, None]).astype(bf16), k))
 
-    grads = ()
+    groups = []
     half = cap // 2
     for k in range(experts):
         a = gathered[k]
         bx, by = over_x(a), over_y(a)
         low, high = over_y(bx[:half]), over_x(by[half:])
-        blocks = (
+        groups.append((
             a, over_core(a), by, over_core(by),
             bx, over_core(bx), low, high, over_core(low), over_core(high),
-        )
+        ))
+    grads = ()
+    for at in range(experts // 2):
+        pair = (2 * at, 2 * at + 1)
         scalars = jnp.stack(
-            [x * width, (1 - x) * width, (z - k) % experts] + [(t ^ r) * cap for r in range(4)]
+            [x * width, (1 - x) * width]
+            + [(t ^ r) * cap for r in range(4)]
+            + [(z - k) % experts for k in pair]
         ).astype(jnp.int32)
-        grads = act_call(k, scalars, blocks, w_down, saved_gate, saved_up, grads)
+        grads = act_call(
+            at, 0, saved_gate.shape[2] // TILE, scalars, [groups[k] for k in pair],
+            w_down, saved_gate, saved_up, grads, (),
+        )
     gg, gu = grads
 
     columns = width // COLUMN_PARTS
     starts = jnp.stack([x, 1 - x]).astype(jnp.int32) * (width // TILE)
     cut = experts // 2 * cap
     hidden_parts, head_rows = [], []
+    sums, outgoing = [], []
     for part in range(COLUMN_PARTS):
-        keep, send = grad_call(part, columns, starts, gg, gu, w_gate, w_up, cap)
+        after = sums[part - 2:part - 1] if part >= 2 else []
+        if part >= 3:
+            after = [*after, *outgoing[part - 3]]
+        keep, send = grad_call(part, columns, starts, gg, gu, w_gate, w_up, cap, after)
         both = (keep.astype(f32) + over_core(send).astype(f32)).astype(bf16)
+        sums.append(both)
         via_x, via_y = over_x(both[1, 1, :cut]), over_y(both[1, 1, cut:])
         to_y = jnp.concatenate(
             [(both[0, 1, :cut].astype(f32) + via_x.astype(f32)).astype(bf16), both[0, 1, cut:]]
@@ -180,6 +204,7 @@
         to_x = jnp.concatenate(
             [both[1, 0, :cut], (both[1, 0, cut:].astype(f32) + via_y.astype(f32)).astype(bf16)]
         )
+        outgoing.append((to_x, to_y))
         from_x, from_y = over_x(to_x), over_y(to_y)
         own = (both[0, 0].astype(f32) + from_x.astype(f32) + from_y.astype(f32)).astype(bf16)
         back = [over_z(own[k * cap:(k + 1) * cap], -k) for k in range(experts)]

time: 365 us -> 369 us (1.011)
  waiting for transfers between devices: 85.2 us -> 144 us
  starting transfers between devices: 97 us -> 64.7 us
  Pallas kernels: 140 us -> 121 us
  local copies, waits for them, and re-layouts: 18.5 us -> 12.7 us
    ppermute x15, waiting for transfers between devices: 11.5 us -> 65.2 us  [over_z(): lax.ppermute(v, 'expert', [(i, (i + shift) % experts) for i in range(expe...]
    ppermute x15, starting transfers between devices: 49.6 us -> 20.4 us  [over_z(): lax.ppermute(v, 'expert', [(i, (i + shift) % experts) for i in range(expe...]
    pallas_call x4 -> x2, Pallas kernels: 62.5 us -> 42.6 us  [act_call(): pl.pallas_call(functools.partial(act_kernel, cap, width, len(groups)), ou...]
    ppermute x20, waiting for transfers between devices: 22.2 us -> 32.4 us  [over_y(): return lax.ppermute(v, 'tp', [(i, i ^ 2) for i in range(4)])]
    ppermute x17, waiting for transfers between devices: 51.3 us -> 46.1 us  [over_x(): return lax.ppermute(v, 'etp', [(0, 1), (1, 0)])]
    unnamed x58 -> x72, local copies, waits for them, and re-layouts: 13.2 us -> 8.49 us
  transfers between devices with their start and end apart: 84 -> 84, of which waited for: 20 -> 30; matrix products, arithmetic and copies ran while one was open for 5% -> 6% of each run, Pallas kernels for 23% -> 22%
where the time goes in v3:
time: 369 us
  waiting for transfers between devices  144 us (39%)
  Pallas kernels  121 us (33%)
  starting transfers between devices  64.7 us (18%)
  local copies, waits for them, and re-layouts  12.7 us (3%)
  matrix products  12.3 us (3%)
  other arithmetic  12.1 us (3%)
    pallas_call x4, Pallas kernels, grad_call(): pl.pallas_call(functools.partial(grad_kernel, cap, experts), out_shape=[j...  78.5 us
    ppermute x15, waiting for transfers between devices, over_z(): lax.ppermute(v, 'expert', [(i, (i + shift) % experts) for i in range(expe...  65.2 us
    ppermute x17, waiting for transfers between devices, over_x(): return lax.ppermute(v, 'etp', [(0, 1), (1, 0)])  46.1 us
    pallas_call x2, Pallas kernels, act_call(): pl.pallas_call(functools.partial(act_kernel, cap, width, len(groups)), ou...  42.6 us
    ppermute x20, waiting for transfers between devices, over_y(): return lax.ppermute(v, 'tp', [(i, i ^ 2) for i in range(4)])  32.4 us
    ppermute x20, starting transfers between devices, over_y(): return lax.ppermute(v, 'tp', [(i, i ^ 2) for i in range(4)])  20.4 us
    ppermute x15, starting transfers between devices, over_z(): lax.ppermute(v, 'expert', [(i, (i + shift) % experts) for i in range(expe...  20.4 us
    ppermute x17, starting transfers between devices, over_x(): return lax.ppermute(v, 'etp', [(0, 1), (1, 0)])  18.9 us
  transfers between devices with their start and end apart: 84, of which 30 were waited for; matrix products, arithmetic and copies ran while one was open for 6% of the time, Pallas kernels for 22%

profile of v3, /device:TPU:0, one launch (start us, length us, event | category | flops | bytes accessed | tf_op | source)
XLA Modules:
  0.0 368.9 jit_solution(15182340130434346662)
XLA Ops:
  4.7 3.0 collective-permute-start.23
  14.8 24.0 %collective-permute-done.refs_0_ = bf16[64,3072]{1,0:T(8,128)(2,1)S(1)} collective-permute-done((bf16[64,3072]{1,0:T(8,128)(2,1)S(1)}, bf16[64,3072]{1,0:T(8,128)(2,1)S(1)}, u32[]{:S(2)}, u32[]{:S(2)}) %collective-permute-start) | collective-permute-done | bytes 393248 | tf_op jit(solution)/shard_map/ppermute | solution.py:135
  43.1 4.1 %collective-permute-done.25.refs_6_ = bf16[32,3072]{1,0:T(8,128)(2,1)S(1)} collective-permute-done((bf16[32,3072]{1,0:T(8,128)(2,1)S(1)}, bf16[32,3072]{1,0:T(8,128)(2,1)S(1)}, u32[]{:S(2)}, u32[]{:S(2)}) %collective-permute-start.25) | collective-permute-done | bytes 196640 | tf_op jit(solution)/shard_map/ppermute | solution.py:141
  48.7 6.3 %collective-permute-done.26.refs_7_ = bf16[32,3072]{1,0:T(8,128)(2,1)S(1)} collective-permute-done((bf16[32,3072]{1,0:T(8,128)(2,1)S(1)}, bf16[32,3072]{1,0:T(8,128)(2,1)S(1)}, u32[]{:S(2)}, u32[]{:S(2)}) %collective-permute-start.26) | collective-permute-done | bytes 196640 | tf_op jit(solution)/shard_map/ppermute | solution.py:138
  57.6 5.8 %collective-permute-done.14.refs_14_ = bf16[64,3072]{1,0:T(8,128)(2,1)S(1)} collective-permute-done((bf16[64,3072]{1,0:T(8,128)(2,1)S(1)}, bf16[64,3072]{1,0:T(8,128)(2,1)S(1)}, u32[]{:S(2)}, u32[]{:S(2)}) %collective-permute-start.14) | collective-permute-done | bytes 393248 | tf_op jit(solution)/shard_map/ppermute | solution.py:138
  63.4 3.6 collective-permute-done.12.refs_12_
  67.5 4.0 %collective-permute-done.33.refs_14_ = bf16[64,3072]{1,0:T(8,128)(2,1)} collective-permute-done((bf16[64,3072]{1,0:T(8,128)(2,1)S(1)}, bf16[64,3072]{1,0:T(8,128)(2,1)}, u32[]{:S(2)}, u32[]{:S(2)}) %collective-permute-start.33) | collective-permute-done | bytes 393248 | tf_op jit(solution)/shard_map/ppermute | solution.py:138
  87.0 2.7 collective-permute-done.35.refs_16_
  99.2 21.5 %act.2 = (bf16[1024,2048]{1,0:T(8,128)(2,1)}, bf16[1024,2048]{1,0:T(8,128)(2,1)}) custom-call(s32[8]{0:T(128)S(1)} %stack.65.s_ref, bf16[64,3072]{1,0:T(8,128)(2,1)S(1)} %fusion.2.refs_0_, bf16[64,3072]{1,0:T(8,128)(2,1)S(1)} %collective-permute-done.20.refs_1_, bf16[64,3072]{1,0:T(8,128)(2,1)S(1)} %collective-permute-done.21.refs_2_, ...), custom_call_target="tpu_custom_call" | custom-call | flops 12884901888 | bytes 39845888 | tf_op jit(solution)/shard_map/act/pallas_call | solution.py:65
  121.6 21.2 %act.3 = (bf16[1024,2048]{1,0:T(8,128)(2,1)}, bf16[1024,2048]{1,0:T(8,128)(2,1)}) custom-call(s32[8]{0:T(128)S(1)} %stack.62.s_ref, bf16[64,3072]{1,0:T(8,128)(2,1)S(1)} %collective-permute-done.refs_0_, bf16[64,3072]{1,0:T(8,128)(2,1)S(1)} %collective-permute-done.1.refs_1_, ...), custom_call_target="tpu_custom_call", output_to_operand_aliasing={{0}: (26, {}), {1}: (27, {})} | custom-call | flops 12884901888 | bytes 39845888 | tf_op jit(solution)/shard_map/act/pallas_call | solution.py:65
  142.8 19.9 %grad.5 = (bf16[2,2,256,768]{3,2,1,0:T(8,128)(2,1)S(1)}, bf16[2,2,256,768]{3,2,1,0:T(8,128)(2,1)}) custom-call(s32[2]{0:T(128)S(1)} %add_multiply_fusion.s_ref, bf16[1024,2048]{1,0:T(8,128)(2,1)} %get-tuple-element.16.gg, bf16[1024,2048]{1,0:T(8,128)(2,1)} %get-tuple-element.17.gu, bf16[1,6144,2048]{2,1,0:T(8,128)(2,1)} %wg.7, bf16[1,6144,2048]{2,1,0:T(8,128)(2,1)} %wu.7), custom_call_target="tpu_custom_call" | custom-call | flops 12884901888 | bytes 24117248 | tf_op jit(solution)/shard_map/grad/pallas_call | solution.py:105
  162.8 19.9 %grad.4 = (bf16[2,2,256,768]{3,2,1,0:T(8,128)(2,1)S(1)}, bf16[2,2,256,768]{3,2,1,0:T(8,128)(2,1)}) custom-call(s32[2]{0:T(128)S(1)} %add_multiply_fusion.s_ref, bf16[1024,2048]{1,0:T(8,128)(2,1)} %get-tuple-element.16.gg, bf16[1024,2048]{1,0:T(8,128)(2,1)} %get-tuple-element.17.gu, bf16[1,6144,2048]{2,1,0:T(8,128)(2,1)} %wg.7, bf16[1,6144,2048]{2,1,0:T(8,128)(2,1)} %wu.7), custom_call_target="tpu_custom_call" | custom-call | flops 12884901888 | bytes 24117248 | tf_op jit(solution)/shard_map/grad/pallas_call | solution.py:105
  187.0 2.9 add_convert_fusion.3.refs_0_
  189.9 19.3 %grad.6 = (bf16[2,2,256,768]{3,2,1,0:T(8,128)(2,1)S(1)}, bf16[2,2,256,768]{3,2,1,0:T(8,128)(2,1)S(1)}) custom-call(s32[2]{0:T(128)S(1)} %add_multiply_fusion.s_ref, bf16[1024,2048]{1,0:T(8,128)(2,1)} %get-tuple-element.16.gg, bf16[1024,2048]{1,0:T(8,128)(2,1)} %get-tuple-element.17.gu, bf16[1,6144,2048]{2,1,0:T(8,128)(2,1)} %wg.7, ...), custom_call_target="tpu_custom_call" | custom-call | flops 12884901888 | bytes 24117248 | tf_op jit(solution)/shard_map/grad/pallas_call | solution.py:105
  215.9 2.7 collective-permute-done.40
  220.4 19.5 %grad.7 = (bf16[2,2,256,768]{3,2,1,0:T(8,128)(2,1)S(1)}, bf16[2,2,256,768]{3,2,1,0:T(8,128)(2,1)S(1)}) custom-call(s32[2]{0:T(128)S(1)} %add_multiply_fusion.s_ref, bf16[1024,2048]{1,0:T(8,128)(2,1)} %get-tuple-element.16.gg, bf16[1024,2048]{1,0:T(8,128)(2,1)} %get-tuple-element.17.gu, bf16[1,6144,2048]{2,1,0:T(8,128)(2,1)} %wg.7, ...), custom_call_target="tpu_custom_call" | custom-call | flops 12884901888 | bytes 24117248 | tf_op jit(solution)/shard_map/grad/pallas_call | solution.py:105
  245.6 7.3 %collective-permute-done.52 = bf16[64,768]{1,0:T(8,128)(2,1)S(1)} collective-permute-done((bf16[64,768]{1,0:T(8,128)(2,1)S(1)}, bf16[64,768]{1,0:T(8,128)(2,1)S(1)}, u32[]{:S(2)}, u32[]{:S(2)}) %collective-permute-start.52) | collective-permute-done | bytes 98336 | tf_op jit(solution)/shard_map/ppermute | solution.py:135
  254.8 2.9 collective-permute-start.44
  258.0 4.2 %collective-permute-done.44 = bf16[64,768]{1,0:T(8,128)(2,1)S(1)} collective-permute-done((bf16[64,768]{1,0:T(8,128)(2,1)S(1)}, bf16[64,768]{1,0:T(8,128)(2,1)S(1)}, u32[]{:S(2)}, u32[]{:S(2)}) %collective-permute-start.44) | collective-permute-done | bytes 98336 | tf_op jit(solution)/shard_map/ppermute | solution.py:135
  266.7 3.5 collective-permute-done.58
  270.2 3.0 collective-permute-done.56
  278.4 5.7 %collective-permute-done.66 = bf16[128,768]{1,0:T(8,128)(2,1)S(1)} collective-permute-done((bf16[128,768]{1,0:T(8,128)(2,1)S(1)}, bf16[128,768]{1,0:T(8,128)(2,1)S(1)}, u32[]{:S(2)}, u32[]{:S(2)}) %collective-permute-start.66) | collective-permute-done | bytes 196640 | tf_op jit(solution)/shard_map/ppermute | solution.py:138
  285.8 4.5 %collective-permute-start.60 = (bf16[64,768]{1,0:T(8,128)(2,1)S(1)}, bf16[64,768]{1,0:T(8,128)(2,1)S(1)}, u32[]{:S(2)}, u32[]{:S(2)}) collective-permute-start(bf16[64,768]{1,0:T(8,128)(2,1)S(1)} %get-tuple-element.60), channel_id=1, source_target_pairs={{0,24},{8,0},{16,8},{24,16},{1,25},{9,1},{17,9},{25,17},{2,26},{10... | collective-permute-start | bytes 294920 | tf_op jit(solution)/shard_map/ppermute | solution.py:135
  291.2 3.5 collective-permute-done.60
  297.0 4.1 %collective-permute-done.62 = bf16[64,768]{1,0:T(8,128)(2,1)S(1)} collective-permute-done((bf16[64,768]{1,0:T(8,128)(2,1)S(1)}, bf16[64,768]{1,0:T(8,128)(2,1)S(1)}, u32[]{:S(2)}, u32[]{:S(2)}) %collective-permute-start.62) | collective-permute-done | bytes 98336 | tf_op jit(solution)/shard_map/ppermute | solution.py:135
  302.3 4.5 %collective-permute-done.72 = bf16[128,768]{1,0:T(8,128)(2,1)S(1)} collective-permute-done((bf16[128,768]{1,0:T(8,128)(2,1)S(1)}, bf16[128,768]{1,0:T(8,128)(2,1)S(1)}, u32[]{:S(2)}, u32[]{:S(2)}) %collective-permute-start.72) | collective-permute-done | bytes 196640 | tf_op jit(solution)/shard_map/ppermute | solution.py:141
  307.5 7.0 %collective-permute-done.61 = bf16[64,768]{1,0:T(8,128)(2,1)S(1)} collective-permute-done((bf16[64,768]{1,0:T(8,128)(2,1)S(1)}, bf16[64,768]{1,0:T(8,128)(2,1)S(1)}, u32[]{:S(2)}, u32[]{:S(2)}) %collective-permute-start.61) | collective-permute-done | bytes 98336 | tf_op jit(solution)/shard_map/ppermute | solution.py:135
  315.9 3.3 collective-permute-done.68
  319.7 6.5 %collective-permute-done.70 = bf16[64,768]{1,0:T(8,128)(2,1)S(1)} collective-permute-done((bf16[64,768]{1,0:T(8,128)(2,1)S(1)}, bf16[64,768]{1,0:T(8,128)(2,1)S(1)}, u32[]{:S(2)}, u32[]{:S(2)}) %collective-permute-start.70) | collective-permute-done | bytes 98336 | tf_op jit(solution)/shard_map/ppermute | solution.py:135
  326.5 5.2 %collective-permute-done.69 = bf16[64,768]{1,0:T(8,128)(2,1)S(1)} collective-permute-done((bf16[64,768]{1,0:T(8,128)(2,1)S(1)}, bf16[64,768]{1,0:T(8,128)(2,1)S(1)}, u32[]{:S(2)}, u32[]{:S(2)}) %collective-permute-start.69) | collective-permute-done | bytes 98336 | tf_op jit(solution)/shard_map/ppermute | solution.py:135
  334.2 4.6 %collective-permute-done.78 = bf16[128,768]{1,0:T(8,128)(2,1)S(1)} collective-permute-done((bf16[128,768]{1,0:T(8,128)(2,1)S(1)}, bf16[128,768]{1,0:T(8,128)(2,1)S(1)}, u32[]{:S(2)}, u32[]{:S(2)}) %collective-permute-start.78) | collective-permute-done | bytes 196640 | tf_op jit(solution)/shard_map/ppermute | solution.py:141
  348.2 18.2 %collective-permute-done.83 = bf16[256,1536]{1,0:T(8,128)(2,1)} collective-permute-done((bf16[256,1536]{1,0:T(8,128)(2,1)S(1)}, bf16[256,1536]{1,0:T(8,128)(2,1)}, u32[]{:S(2)}, u32[]{:S(2)}) %collective-permute-start.83) | collective-permute-done | bytes 786464 | tf_op jit(solution)/shard_map/ppermute | solution.py:138
  (297 shorter events, 98.9 us)
Async XLA Ops:
  4.7 34.1 %collective-permute-start.23 = (bf16[64,3072]{1,0:T(8,128)(2,1)S(1)}, bf16[64,3072]{1,0:T(8,128)(2,1)S(1)}, u32[]{:S(2)}, u32[]{:S(2)}) collective-permute-start(bf16[64,3072]{1,0:T(8,128)(2,1)S(1)} %fusion.2.refs_0_), channel_id=1, source_target_pairs={{0,4},{4,0},{1,5},{5,1},{2,6},{6,2},{3,7},{7,3},{8,12},{12,8},{9,1... | collective-permute-start | bytes 1179656 | tf_op jit(solution)/shard_map/ppermute | solution.py:138
  7.7 31.7 %collective-permute-start.21 = (bf16[64,3072]{1,0:T(8,128)(2,1)S(1)}, bf16[64,3072]{1,0:T(8,128)(2,1)S(1)}, u32[]{:S(2)}, u32[]{:S(2)}) collective-permute-start(bf16[64,3072]{1,0:T(8,128)(2,1)S(1)} %fusion.2.refs_0_), channel_id=1, source_target_pairs={{0,2},{1,3},{2,0},{3,1},{4,6},{5,7},{6,4},{7,5},{8,10},{9,11},{10,... | collective-permute-start | bytes 1179656 | tf_op jit(solution)/shard_map/ppermute | solution.py:141
  9.4 29.3 %collective-permute-start = (bf16[64,3072]{1,0:T(8,128)(2,1)S(1)}, bf16[64,3072]{1,0:T(8,128)(2,1)S(1)}, u32[]{:S(2)}, u32[]{:S(2)}) collective-permute-start(bf16[64,3072]{1,0:T(8,128)(2,1)S(1)} %fusion), channel_id=1, source_target_pairs={{0,16},{8,24},{16,0},{24,8},{1,17},{9,25},{17,1},{25,9},{2,18},{10... | collective-permute-start | bytes 1179656 | tf_op jit(solution)/shard_map/ppermute | solution.py:135
  12.4 27.6 %collective-permute-start.10 = (bf16[64,3072]{1,0:T(8,128)(2,1)S(1)}, bf16[64,3072]{1,0:T(8,128)(2,1)S(1)}, u32[]{:S(2)}, u32[]{:S(2)}) collective-permute-start(bf16[64,3072]{1,0:T(8,128)(2,1)S(1)} %fusion.1), channel_id=1, source_target_pairs={{0,24},{8,0},{16,8},{24,16},{1,25},{9,1},{17,9},{25,17},{2,26},{10... | collective-permute-start | bytes 1179656 | tf_op jit(solution)/shard_map/ppermute | solution.py:135
  14.0 27.5 %collective-permute-start.29 = (bf16[64,3072]{1,0:T(8,128)(2,1)S(1)}, bf16[64,3072]{1,0:T(8,128)(2,1)S(1)}, u32[]{:S(2)}, u32[]{:S(2)}) collective-permute-start(bf16[64,3072]{1,0:T(8,128)(2,1)S(1)} %fusion.3), channel_id=1, source_target_pairs={{0,8},{8,16},{16,24},{24,0},{1,9},{9,17},{17,25},{25,1},{2,10},{10... | collective-permute-start | bytes 1179656 | tf_op jit(solution)/shard_map/ppermute | solution.py:135
  38.8 16.6 %collective-permute-start.4 = (bf16[64,3072]{1,0:T(8,128)(2,1)S(1)}, bf16[64,3072]{1,0:T(8,128)(2,1)S(1)}, u32[]{:S(2)}, u32[]{:S(2)}) collective-permute-start(bf16[64,3072]{1,0:T(8,128)(2,1)S(1)} %collective-permute-done.refs_0_), channel_id=1, source_target_pairs={{0,4},{4,0},{1,5},{5,1},{2,6},{6,2},{3,7},{7,3},{8,12},{12,8},{9,1... | collective-permute-start | bytes 1179656 | tf_op jit(solution)/shard_map/ppermute | solution.py:138
  47.2 16.2 %collective-permute-start.14 = (bf16[64,3072]{1,0:T(8,128)(2,1)S(1)}, bf16[64,3072]{1,0:T(8,128)(2,1)S(1)}, u32[]{:S(2)}, u32[]{:S(2)}) collective-permute-start(bf16[64,3072]{1,0:T(8,128)(2,1)S(1)} %collective-permute-done.10.refs_10_), channel_id=1, source_target_pairs={{0,4},{4,0},{1,5},{5,1},{2,6},{6,2},{3,7},{7,3},{8,12},{12,8},{9,1... | collective-permute-start | bytes 1179656 | tf_op jit(solution)/shard_map/ppermute | solution.py:138
  55.4 16.0 %collective-permute-start.33 = (bf16[64,3072]{1,0:T(8,128)(2,1)S(1)}, bf16[64,3072]{1,0:T(8,128)(2,1)}, u32[]{:S(2)}, u32[]{:S(2)}) collective-permute-start(bf16[64,3072]{1,0:T(8,128)(2,1)S(1)} %collective-permute-done.29.refs_10_), channel_id=1, source_target_pairs={{0,4},{4,0},{1,5},{5,1},{2,6},{6,2},{3,7},{7,3},{8,12},{12,8},{9,1... | collective-permute-start | bytes 1179656 | tf_op jit(solution)/shard_map/ppermute | solution.py:138
  56.4 17.4 %collective-permute-start.31 = (bf16[64,3072]{1,0:T(8,128)(2,1)S(1)}, bf16[64,3072]{1,0:T(8,128)(2,1)}, u32[]{:S(2)}, u32[]{:S(2)}) collective-permute-start(bf16[64,3072]{1,0:T(8,128)(2,1)S(1)} %collective-permute-done.29.refs_10_), channel_id=1, source_target_pairs={{0,2},{1,3},{2,0},{3,1},{4,6},{5,7},{6,4},{7,5},{8,10},{9,11},{10,... | collective-permute-start | bytes 1179656 | tf_op jit(solution)/shard_map/ppermute | solution.py:141
  92.5 28.1 %collective-permute-start.3 = (bf16[64,3072]{1,0:T(8,128)(2,1)S(1)}, bf16[64,3072]{1,0:T(8,128)(2,1)S(1)}, u32[]{:S(2)}, u32[]{:S(2)}) collective-permute-start(bf16[64,3072]{1,0:T(8,128)(2,1)S(1)} %collective-permute-done.2.refs_2_), channel_id=1, source_target_pairs={{0,1},{1,0},{2,3},{3,2},{4,5},{5,4},{6,7},{7,6},{8,9},{9,8},{10,11... | collective-permute-start | bytes 1179656 | tf_op jit(solution)/shard_map/ppermute | solution.py:144
  92.9 27.8 %collective-permute-start.15 = (bf16[64,3072]{1,0:T(8,128)(2,1)}, bf16[64,3072]{1,0:T(8,128)(2,1)S(1)}, u32[]{:S(2)}, u32[]{:S(2)}) collective-permute-start(bf16[64,3072]{1,0:T(8,128)(2,1)} %copy-done.26), channel_id=1, source_target_pairs={{0,1},{1,0},{2,3},{3,2},{4,5},{5,4},{6,7},{7,6},{8,9},{9,8},{10,11... | collective-permute-start | bytes 1179656 | tf_op jit(solution)/shard_map/ppermute | solution.py:144
  93.1 27.6 %collective-permute-start.13 = (bf16[64,3072]{1,0:T(8,128)(2,1)}, bf16[64,3072]{1,0:T(8,128)(2,1)S(1)}, u32[]{:S(2)}, u32[]{:S(2)}) collective-permute-start(bf16[64,3072]{1,0:T(8,128)(2,1)} %copy-done.27), channel_id=1, source_target_pairs={{0,1},{1,0},{2,3},{3,2},{4,5},{5,4},{6,7},{7,6},{8,9},{9,8},{10,11... | collective-permute-start | bytes 1179656 | tf_op jit(solution)/shard_map/ppermute | solution.py:144
  93.9 26.7 %collective-permute-start.18 = (bf16[32,3072]{1,0:T(8,128)(2,1)}, bf16[32,3072]{1,0:T(8,128)(2,1)S(1)}, u32[]{:S(2)}, u32[]{:S(2)}) collective-permute-start(bf16[32,3072]{1,0:T(8,128)(2,1)} %copy-done.14), channel_id=1, source_target_pairs={{0,1},{1,0},{2,3},{3,2},{4,5},{5,4},{6,7},{7,6},{8,9},{9,8},{10,11... | collective-permute-start | bytes 589832 | tf_op jit(solution)/shard_map/ppermute | solution.py:144
  94.1 26.6 %collective-permute-start.19 = (bf16[32,3072]{1,0:T(8,128)(2,1)}, bf16[32,3072]{1,0:T(8,128)(2,1)S(1)}, u32[]{:S(2)}, u32[]{:S(2)}) collective-permute-start(bf16[32,3072]{1,0:T(8,128)(2,1)} %copy-done.16), channel_id=1, source_target_pairs={{0,1},{1,0},{2,3},{3,2},{4,5},{5,4},{6,7},{7,6},{8,9},{9,8},{10,11... | collective-permute-start | bytes 589832 | tf_op jit(solution)/shard_map/ppermute | solution.py:144
  162.7 20.4 %collective-permute-start.47 = (bf16[2,2,256,768]{3,2,1,0:T(8,128)(2,1)}, bf16[2,2,256,768]{3,2,1,0:T(8,128)(2,1)}, u32[]{:S(2)}, u32[]{:S(2)}) collective-permute-start(bf16[2,2,256,768]{3,2,1,0:T(8,128)(2,1)} %get-tuple-element.21), channel_id=1, source_target_pairs={{0,1},{1,0},{2,3},{3,2},{4,5},{5,4},{6,7},{7,6},{8,9},{9,8},{10,11... | collective-permute-start | bytes 4718600 | tf_op jit(solution)/shard_map/ppermute | solution.py:144
  184.9 26.5 %collective-permute-start.50 = (bf16[128,768]{1,0:T(8,128)(2,1)S(1)}, bf16[128,768]{1,0:T(8,128)(2,1)S(1)}, u32[]{:S(2)}, u32[]{:S(2)}) collective-permute-start(bf16[128,768]{1,0:T(8,128)(2,1)S(1)} %get-tuple-element.28), channel_id=1, source_target_pairs={{0,4},{4,0},{1,5},{5,1},{2,6},{6,2},{3,7},{7,3},{8,12},{12,8},{9,1... | collective-permute-start | bytes 589832 | tf_op jit(solution)/shard_map/ppermute | solution.py:138
  185.5 25.9 %collective-permute-start.48 = (bf16[128,768]{1,0:T(8,128)(2,1)S(1)}, bf16[128,768]{1,0:T(8,128)(2,1)S(1)}, u32[]{:S(2)}, u32[]{:S(2)}) collective-permute-start(bf16[128,768]{1,0:T(8,128)(2,1)S(1)} %get-tuple-element.29), channel_id=1, source_target_pairs={{0,2},{1,3},{2,0},{3,1},{4,6},{5,7},{6,4},{7,5},{8,10},{9,11},{10,... | collective-permute-start | bytes 589832 | tf_op jit(solution)/shard_map/ppermute | solution.py:141
  211.4 52.6 %collective-permute-start.55 = (bf16[2,2,256,768]{3,2,1,0:T(8,128)(2,1)S(1)}, bf16[2,2,256,768]{3,2,1,0:T(8,128)(2,1)S(1)}, u32[]{:S(2)}, u32[]{:S(2)}) collective-permute-start(bf16[2,2,256,768]{3,2,1,0:T(8,128)(2,1)S(1)} %get-tuple-element.23), channel_id=1, source_target_pairs={{0,1},{1,0},{2,3},{3,2},{4,5},{5,4},{6,7},{7,6},{8,9},{9,8},{10,11... | collective-permute-start | bytes 4718600 | tf_op jit(solution)/shard_map/ppermute | solution.py:144
  211.5 28.4 %collective-permute-start.51 = (bf16[256,768]{1,0:T(8,128)(2,1)S(1)}, bf16[256,768]{1,0:T(8,128)(2,1)S(1)}, u32[]{:S(2)}, u32[]{:S(2)}) collective-permute-start(bf16[256,768]{1,0:T(8,128)(2,1)S(1)} %pad_maximum_fusion.4), channel_id=1, source_target_pairs={{0,2},{1,3},{2,0},{3,1},{4,6},{5,7},{6,4},{7,5},{8,10},{9,11},{10,... | collective-permute-start | bytes 1179656 | tf_op jit(solution)/shard_map/ppermute | solution.py:141
  213.1 26.8 %collective-permute-start.49 = (bf16[256,768]{1,0:T(8,128)(2,1)S(1)}, bf16[256,768]{1,0:T(8,128)(2,1)S(1)}, u32[]{:S(2)}, u32[]{:S(2)}) collective-permute-start(bf16[256,768]{1,0:T(8,128)(2,1)S(1)} %pad_maximum_fusion.3), channel_id=1, source_target_pairs={{0,4},{4,0},{1,5},{5,1},{2,6},{6,2},{3,7},{7,3},{8,12},{12,8},{9,1... | collective-permute-start | bytes 1179656 | tf_op jit(solution)/shard_map/ppermute | solution.py:138
  218.8 22.7 %collective-permute-start.41 = (bf16[256,768]{1,0:T(8,128)(2,1)S(1)}, bf16[256,768]{1,0:T(8,128)(2,1)S(1)}, u32[]{:S(2)}, u32[]{:S(2)}) collective-permute-start(bf16[256,768]{1,0:T(8,128)(2,1)S(1)} %pad_maximum_fusion.1.refs_1_), channel_id=1, source_target_pairs={{0,4},{4,0},{1,5},{5,1},{2,6},{6,2},{3,7},{7,3},{8,12},{12,8},{9,1... | collective-permute-start | bytes 1179656 | tf_op jit(solution)/shard_map/ppermute | solution.py:138
  219.4 24.7 %collective-permute-start.43 = (bf16[256,768]{1,0:T(8,128)(2,1)S(1)}, bf16[256,768]{1,0:T(8,128)(2,1)S(1)}, u32[]{:S(2)}, u32[]{:S(2)}) collective-permute-start(bf16[256,768]{1,0:T(8,128)(2,1)S(1)} %pad_maximum_fusion.2.refs_2_), channel_id=1, source_target_pairs={{0,2},{1,3},{2,0},{3,1},{4,6},{5,7},{6,4},{7,5},{8,10},{9,11},{10,... | collective-permute-start | bytes 1179656 | tf_op jit(solution)/shard_map/ppermute | solution.py:141
  239.9 35.5 %collective-permute-start.63 = (bf16[2,2,256,768]{3,2,1,0:T(8,128)(2,1)S(1)}, bf16[2,2,256,768]{3,2,1,0:T(8,128)(2,1)S(1)}, u32[]{:S(2)}, u32[]{:S(2)}) collective-permute-start(bf16[2,2,256,768]{3,2,1,0:T(8,128)(2,1)S(1)} %get-tuple-element.25), channel_id=1, source_target_pairs={{0,1},{1,0},{2,3},{3,2},{4,5},{5,4},{6,7},{7,6},{8,9},{9,8},{10,11... | collective-permute-start | bytes 4718600 | tf_op jit(solution)/shard_map/ppermute | solution.py:144
  252.9 23.9 %collective-permute-start.45 = (bf16[64,768]{1,0:T(8,128)(2,1)S(1)}, bf16[64,768]{1,0:T(8,128)(2,1)S(1)}, u32[]{:S(2)}, u32[]{:S(2)}) collective-permute-start(bf16[64,768]{1,0:T(8,128)(2,1)S(1)} %get-tuple-element.52), channel_id=1, source_target_pairs={{0,16},{8,24},{16,0},{24,8},{1,17},{9,25},{17,1},{25,9},{2,18},{10... | collective-permute-start | bytes 294920 | tf_op jit(solution)/shard_map/ppermute | solution.py:135
  262.2 40.0 %collective-permute-start.75 = (bf16[128,768]{1,0:T(8,128)(2,1)S(1)}, bf16[128,768]{1,0:T(8,128)(2,1)S(1)}, u32[]{:S(2)}, u32[]{:S(2)}) collective-permute-start(bf16[128,768]{1,0:T(8,128)(2,1)S(1)} %fusion.23), channel_id=1, source_target_pairs={{0,2},{1,3},{2,0},{3,1},{4,6},{5,7},{6,4},{7,5},{8,10},{9,11},{10,... | collective-permute-start | bytes 589832 | tf_op jit(solution)/shard_map/ppermute | solution.py:141
  284.1 48.7 %collective-permute-start.74 = (bf16[128,768]{1,0:T(8,128)(2,1)S(1)}, bf16[128,768]{1,0:T(8,128)(2,1)S(1)}, u32[]{:S(2)}, u32[]{:S(2)}) collective-permute-start(bf16[128,768]{1,0:T(8,128)(2,1)S(1)} %fusion.23), channel_id=1, source_target_pairs={{0,1},{1,0},{2,3},{3,2},{4,5},{5,4},{6,7},{7,6},{8,9},{9,8},{10,11... | collective-permute-start | bytes 589832 | tf_op jit(solution)/shard_map/ppermute | solution.py:144
  284.4 22.4 %collective-permute-start.67 = (bf16[256,768]{1,0:T(8,128)(2,1)S(1)}, bf16[256,768]{1,0:T(8,128)(2,1)S(1)}, u32[]{:S(2)}, u32[]{:S(2)}) collective-permute-start(bf16[256,768]{1,0:T(8,128)(2,1)S(1)} %pad_maximum_fusion.8), channel_id=1, source_target_pairs={{0,2},{1,3},{2,0},{3,1},{4,6},{5,7},{6,4},{7,5},{8,10},{9,11},{10,... | collective-permute-start | bytes 1179656 | tf_op jit(solution)/shard_map/ppermute | solution.py:141
  290.3 16.9 %collective-permute-start.65 = (bf16[256,768]{1,0:T(8,128)(2,1)S(1)}, bf16[256,768]{1,0:T(8,128)(2,1)S(1)}, u32[]{:S(2)}, u32[]{:S(2)}) collective-permute-start(bf16[256,768]{1,0:T(8,128)(2,1)S(1)} %pad_maximum_fusion.7), channel_id=1, source_target_pairs={{0,4},{4,0},{1,5},{5,1},{2,6},{6,2},{3,7},{7,3},{8,12},{12,8},{9,1... | collective-permute-start | bytes 1179656 | tf_op jit(solution)/shard_map/ppermute | solution.py:138
  302.2 42.3 %collective-permute-start.71 = (bf16[128,768]{1,0:T(8,128)(2,1)S(1)}, bf16[128,768]{1,0:T(8,128)(2,1)S(1)}, u32[]{:S(2)}, u32[]{:S(2)}) collective-permute-start(bf16[128,768]{1,0:T(8,128)(2,1)S(1)} %fusion.22), channel_id=1, source_target_pairs={{0,1},{1,0},{2,3},{3,2},{4,5},{5,4},{6,7},{7,6},{8,9},{9,8},{10,11... | collective-permute-start | bytes 589832 | tf_op jit(solution)/shard_map/ppermute | solution.py:144
  306.8 26.2 %collective-permute-start.76 = (bf16[128,768]{1,0:T(8,128)(2,1)S(1)}, bf16[128,768]{1,0:T(8,128)(2,1)S(1)}, u32[]{:S(2)}, u32[]{:S(2)}) collective-permute-start(bf16[128,768]{1,0:T(8,128)(2,1)S(1)} %collective-permute-done.75), channel_id=1, source_target_pairs={{0,1},{1,0},{2,3},{3,2},{4,5},{5,4},{6,7},{7,6},{8,9},{9,8},{10,11... | collective-permute-start | bytes 589832 | tf_op jit(solution)/shard_map/ppermute | solution.py:144
  306.8 37.8 %collective-permute-start.73 = (bf16[128,768]{1,0:T(8,128)(2,1)S(1)}, bf16[128,768]{1,0:T(8,128)(2,1)S(1)}, u32[]{:S(2)}, u32[]{:S(2)}) collective-permute-start(bf16[128,768]{1,0:T(8,128)(2,1)S(1)} %collective-permute-done.72), channel_id=1, source_target_pairs={{0,1},{1,0},{2,3},{3,2},{4,5},{5,4},{6,7},{7,6},{8,9},{9,8},{10,11... | collective-permute-start | bytes 589832 | tf_op jit(solution)/shard_map/ppermute | solution.py:144
  346.2 20.1 %collective-permute-start.83 = (bf16[256,1536]{1,0:T(8,128)(2,1)S(1)}, bf16[256,1536]{1,0:T(8,128)(2,1)}, u32[]{:S(2)}, u32[]{:S(2)}) collective-permute-start(bf16[256,1536]{1,0:T(8,128)(2,1)S(1)} %broadcast_select_fusion), channel_id=1, source_target_pairs={{0,4},{4,0},{1,5},{5,1},{2,6},{6,2},{3,7},{7,3},{8,12},{12,8},{9,1... | collective-permute-start | bytes 2359304 | tf_op jit(solution)/shard_map/ppermute | solution.py:138
  (88 other events, 1035.9 us)
